TPU v7x, 32 devices: a whole 2x2x4 slice. The times are simulated.
32 devices in a mesh: seq: 16 (over z, x, core), batch: 2 (over y).
Axes of the slice: x: 2, y: 2, z: 4, core: 2. Of those that a mesh axis runs over, the one named last changes fastest.
Arguments:
- inputs: bfloat16 [2, 2048, 768], P('batch', 'seq'), may hold values from -6 to 6
- attend_gain: bfloat16 [768], P(('seq', 'batch')), may hold values from 0.5 to 1.5
- attend_shift: bfloat16 [768], P(('seq', 'batch')), may hold values from -0.59765625 to 0.59765625
- mixing_weight: bfloat16 [768, 2304], P(('seq', 'batch')), may hold values from -0.21875 to 0.21875
- mixing_bias: bfloat16 [1536], P(('seq', 'batch')), may hold values from -0.119628906 to 0.119628906
- output_weight: bfloat16 [768, 768], P(('seq', 'batch')), may hold values from -0.875 to 0.875
- output_bias: bfloat16 [768], P(('seq', 'batch')), may hold values from -1.796875 to 1.796875
- feed_gain: bfloat16 [768], P(('seq', 'batch')), may hold values from 0.5 to 1.5
- feed_shift: bfloat16 [768], P(('seq', 'batch')), may hold values from -0.59765625 to 0.59765625
- up_weight: bfloat16 [768, 3072], P(('seq', 'batch')), may hold values from -0.21875 to 0.21875
- up_bias: bfloat16 [3072], P(('seq', 'batch')), may hold values from -0.59765625 to 0.59765625
- down_weight: bfloat16 [3072, 768], P(('seq', 'batch')), may hold values from -0.4375 to 0.4375
- down_bias: bfloat16 [768], P(('seq', 'batch')), may hold values from -2.390625 to 2.390625
- cotangent: bfloat16 [2, 2, 2048, 768], P(None, 'batch', 'seq'), may hold values from -6 to 6
Outputs:
- activations: bfloat16 [2, 2, 2048, 768], P(None, 'batch', 'seq')
- input_gradient: float32 [2, 2, 2048, 768], P(None, 'batch', 'seq')
- attend_gain_gradient: float32 [2, 768], P(None, ('seq', 'batch'))
- attend_shift_gradient: float32 [2, 768], P(None, ('seq', 'batch'))
- mixing_weight_gradient: float32 [2, 768, 2304], P(None, ('seq', 'batch'))
- mixing_bias_gradient: float32 [2, 1536], P(None, ('seq', 'batch'))
- output_weight_gradient: float32 [2, 768, 768], P(None, ('seq', 'batch'))
- output_bias_gradient: float32 [2, 768], P(None, ('seq', 'batch'))
- feed_gain_gradient: float32 [2, 768], P(None, ('seq', 'batch'))
- feed_shift_gradient: float32 [2, 768], P(None, ('seq', 'batch'))
- up_weight_gradient: float32 [2, 768, 3072], P(None, ('seq', 'batch'))
- up_bias_gradient: float32 [2, 3072], P(None, ('seq', 'batch'))
- down_weight_gradient: float32 [2, 3072, 768], P(None, ('seq', 'batch'))
- down_bias_gradient: float32 [2, 768], P(None, ('seq', 'batch'))
All inputs are finite; a program needn't handle non-finite values.
Results may differ from a plain program's by a relative error of at most 0.014.
Values may be sent and summed in bfloat16 or wider, within the bound.
A program may use at most 320 MiB of HBM per device.

v0:
```python
from functools import partial

import jax
import jax.numpy as jnp
from jax import lax
from jax.experimental import pallas as pl
from jax.experimental.pallas import tpu as pltpu
from jax.sharding import PartitionSpec as P

HEADS = 12
EPS = 1e-05
SCALES = (12.0 ** (-0.5), 48.0 ** (-0.5))
NEGATIVE = -1e30
LOW = jnp.bfloat16
FULL = jnp.float32
TILE = 256


def normalize(values):
    average = jnp.mean(values, axis=-1, keepdims=True)
    centered = values - average
    inv_std = lax.rsqrt(jnp.mean(centered * centered, axis=-1, keepdims=True) + EPS)
    return centered * inv_std, inv_std


def norm_back(gradient, normed, inv_std, gain):
    scaled = gradient * gain
    inner = (
        scaled
        - jnp.mean(scaled, axis=-1, keepdims=True)
        - normed * jnp.mean(scaled * normed, axis=-1, keepdims=True)
    )
    return inv_std * inner


def dot(a, b, dims):
    return lax.dot_general(a, b, ((dims[:1], dims[1:]), ((), ())), preferred_element_type=FULL)


class Place:
    def __init__(self):
        self.s = lax.axis_size("seq")
        self.ny = lax.axis_size("batch")
        self.nz = self.s // 4
        seq = lax.axis_index("seq")
        self.y = lax.axis_index("batch")
        self.core = lax.rem(seq, 2)
        self.chip = seq // 2
        self.x = lax.rem(self.chip, 2)
        self.z = self.chip // 2
        self.sizes = {"z": self.nz, "x": 2, "y": self.ny, "core": 2}
        self.at = {"z": self.z, "x": self.x, "y": self.y, "core": self.core}

    def send(self, values, axis, d=1):
        pairs = []
        for s in range(self.s):
            for y in range(self.ny):
                c, x, z, t = s % 2, (s // 2) % 2, s // 4, y
                if axis == "z":
                    z = (z + d) % self.nz
                elif axis == "x":
                    x = 1 - x
                elif axis == "core":
                    c = 1 - c
                else:
                    t = (y + d) % self.ny
                pairs.append((s * self.ny + y, ((z * 2 + x) * 2 + c) * self.ny + t))
        return lax.ppermute(values, ("seq", "batch"), pairs)

    def gather(self, values, axis, dim):
        size, at = self.sizes[axis], self.at[axis]
        shape = values.shape[:dim] + (size,) + values.shape[dim:]
        whole = lax.dynamic_update_slice_in_dim(
            jnp.zeros(shape, values.dtype), jnp.expand_dims(values, dim), at, dim
        )
        for d in range(1, size):
            piece = jnp.expand_dims(self.send(values, axis, d), dim)
            whole = lax.dynamic_update_slice_in_dim(whole, piece, lax.rem(at + size - d, size), dim)
        return whole

    def scatter(self, values, axis, dim):
        size, at = self.sizes[axis], self.at[axis]

        def pick(i):
            return lax.dynamic_index_in_dim(values, lax.rem(i, size), dim, keepdims=False)

        total = pick(at).astype(FULL)
        for d in range(1, size):
            total = total + self.send(pick(at + d), axis, d).astype(FULL)
        return total

    def both(self, mine, theirs):
        got = self.send(theirs, "core")
        first = self.core == 0
        return jnp.stack([jnp.where(first, mine, got), jnp.where(first, got, mine)])


def attend_plain_kernel(x_ref, gain_ref, shift_ref, w_ref, b_ref, h_ref, q_ref, k_ref, v_ref, o_ref, ot_ref, top_ref, vt_ref):
    length = x_ref.shape[0]
    head = q_ref.shape[1]
    tiles = length // TILE

    def project(i, _):
        rows = pl.ds(pl.multiple_of(i * TILE, TILE), TILE)
        normed, _ = normalize(x_ref[rows, :].astype(FULL))
        low = (normed * gain_ref[...] + shift_ref[...]).astype(LOW)
        h_ref[rows, :] = low
        mixed = dot(low, w_ref[...], (1, 0)) + b_ref[...]
        q_ref[rows, :] = (mixed[:, :head].astype(LOW) * (head ** (-0.5))).astype(LOW)
        k_ref[rows, :] = mixed[:, head : 2 * head].astype(LOW)
        value = mixed[:, 2 * head :].astype(LOW)
        v_ref[rows, :] = value
        vt_ref[:, rows] = value.T
        return 0

    lax.fori_loop(0, tiles, project, 0)

    def query_tile(i, _):
        rows = pl.ds(pl.multiple_of(i * TILE, TILE), TILE)
        query = q_ref[rows, :]

        def absorb(j, carry, masked):
            top, total, acc = carry
            keys = pl.ds(pl.multiple_of(j * TILE, TILE), TILE)
            scores = dot(k_ref[keys, :], query, (1, 1))
            if masked:
                key_pos = lax.broadcasted_iota(jnp.int32, scores.shape, 0)
                query_pos = lax.broadcasted_iota(jnp.int32, scores.shape, 1)
                scores = jnp.where(key_pos <= query_pos, scores, NEGATIVE)
            new_top = jnp.maximum(top, jnp.max(scores, axis=0, keepdims=True))
            weights = jnp.exp(scores - new_top)
            keep = jnp.exp(top - new_top)
            total = total * keep + jnp.sum(weights, axis=0, keepdims=True)
            acc = acc * keep + dot(vt_ref[:, keys], weights.astype(LOW), (1, 0))
            return new_top, total, acc

        start = (
            jnp.full((1, TILE), NEGATIVE, FULL),
            jnp.zeros((1, TILE), FULL),
            jnp.zeros((head, TILE), FULL),
        )
        carry = lax.fori_loop(0, i, lambda j, c: absorb(j, c, False), start)
        top, total, acc = absorb(i, carry, True)
        out = acc / total
        ot_ref[:, rows] = out
        o_ref[rows, :] = out.T.astype(LOW)
        top_ref[:, rows] = top + jnp.log(total)
        return 0

    lax.fori_loop(0, tiles, query_tile, 0)


def attend_plain(x_all, gain, shift, weight, bias):
    length, head = x_all.shape[0], weight.shape[1] // 3
    low = jax.ShapeDtypeStruct((length, head), LOW)
    return pl.pallas_call(
        attend_plain_kernel,
        out_shape=(
            jax.ShapeDtypeStruct(x_all.shape, LOW),
            low,
            low,
            low,
            low,
            jax.ShapeDtypeStruct((head, length), FULL),
            jax.ShapeDtypeStruct((1, length), FULL),
        ),
        scratch_shapes=[pltpu.VMEM((head, length), LOW)],
        compiler_params=pltpu.CompilerParams(vmem_limit_bytes=48 << 20),
        cost_estimate=pl.CostEstimate(
            flops=6 * length * length * head, bytes_accessed=8 * length * 768, transcendentals=length * length
        ),
        name="attend_plain",
    )(x_all, gain, shift, weight, bias)


def attend_back_kernel(
    q_ref, k_ref, v_ref, ot_ref, top_ref, go_ref, gq_ref, gk_ref, gv_ref, kt_ref, got_ref, delta_ref, gqt_ref
):
    length, head = q_ref.shape
    tiles = length // TILE
    factor = head ** (-0.5)

    def prepare(i, _):
        rows = pl.ds(pl.multiple_of(i * TILE, TILE), TILE)
        kt_ref[:, rows] = k_ref[rows, :].T
        up = go_ref[rows, :].T
        for d in range(2):
            mine = up[d * head : (d + 1) * head, :]
            got_ref[d, :, rows] = mine
            delta_ref[d, :, rows] = jnp.sum(mine.astype(FULL) * ot_ref[:, rows], axis=0, keepdims=True)
            gqt_ref[d, :, rows] = jnp.zeros((head, TILE), FULL)
        return 0

    lax.fori_loop(0, tiles, prepare, 0)

    def key_tile(j, _):
        keys = pl.ds(pl.multiple_of(j * TILE, TILE), TILE)
        key = k_ref[keys, :]
        value = v_ref[keys, :]
        key_t = kt_ref[:, keys]

        def step(i, carry, masked):
            gv, gk0, gk1 = carry
            rows = pl.ds(pl.multiple_of(i * TILE, TILE), TILE)
            query = q_ref[rows, :]
            scores = dot(key, query, (1, 1))
            if masked:
                key_pos = lax.broadcasted_iota(jnp.int32, scores.shape, 0)
                query_pos = lax.broadcasted_iota(jnp.int32, scores.shape, 1)
                scores = jnp.where(key_pos <= query_pos, scores, NEGATIVE)
            probs = jnp.exp(scores - top_ref[:, rows])
            gv = gv + dot(probs.astype(LOW), go_ref[rows, :], (1, 0))
            gks = [gk0, gk1]
            for d in range(2):
                prob_grad = dot(value, got_ref[d, :, rows], (1, 0))
                score_low = (probs * (prob_grad - delta_ref[d, :, rows])).astype(LOW)
                gks[d] = gks[d] + dot(score_low, query, (1, 0))
                gqt_ref[d, :, rows] += dot(key_t, score_low, (1, 0))
            return gv, gks[0], gks[1]

        zero = jnp.zeros((TILE, head), FULL)
        carry = step(j, (jnp.zeros((TILE, 2 * head), FULL), zero, zero), True)
        gv, gk0, gk1 = lax.fori_loop(j + 1, tiles, lambda i, c: step(i, c, False), carry)
        gv_ref[keys, :] = gv.astype(LOW)
        gk_ref[keys, :] = jnp.concatenate([gk0, gk1], axis=1).astype(LOW)
        return 0

    lax.fori_loop(0, tiles, key_tile, 0)

    def finish(i, _):
        rows = pl.ds(pl.multiple_of(i * TILE, TILE), TILE)
        both = jnp.concatenate([gqt_ref[0, :, rows], gqt_ref[1, :, rows]], axis=0) * factor
        gq_ref[rows, :] = both.T.astype(LOW)
        return 0

    lax.fori_loop(0, tiles, finish, 0)


def attend_back(q, k, v, out_t, top, go):
    length, head = q.shape
    pair = jax.ShapeDtypeStruct((length, 2 * head), LOW)
    return pl.pallas_call(
        attend_back_kernel,
        out_shape=(pair, pair, pair),
        scratch_shapes=[
            pltpu.VMEM((head, length), LOW),
            pltpu.VMEM((2, head, length), LOW),
            pltpu.VMEM((2, 1, length), FULL),
            pltpu.VMEM((2, head, length), FULL),
        ],
        compiler_params=pltpu.CompilerParams(vmem_limit_bytes=48 << 20),
        cost_estimate=pl.CostEstimate(
            flops=20 * length * length * head, bytes_accessed=16 * length * head, transcendentals=length * length
        ),
        name="attend_back",
    )(q, k, v, out_t, top, go)


MESH = pl.DeviceIdType.MESH
DMA = pltpu.SemaphoreType.DMA


class Here:
    def __init__(self, nz, ny):
        self.nz, self.ny = nz, ny
        seq = lax.axis_index("seq")
        self.y = lax.axis_index("batch")
        self.core = lax.rem(seq, 2)
        self.chip = lax.div(seq, 2)
        self.x = lax.rem(self.chip, 2)
        self.z = lax.div(self.chip, 2)

    def device(self, z=None, x=None, core=None, y=None):
        z = self.z if z is None else z
        x = self.x if x is None else x
        core = self.core if core is None else core
        y = self.y if y is None else y
        return ((z * 2 + x) * 2 + core, y)

    def before(self, d):
        return lax.rem(self.z + self.nz - d, self.nz)

    def after(self, d):
        return lax.rem(self.z + d, self.nz)


def remote(src, dst, send, recv, device):
    return pltpu.make_async_remote_copy(
        src_ref=src, dst_ref=dst, send_sem=send, recv_sem=recv, device_id=device, device_id_type=MESH
    )


class Gather:
    def __init__(self, here, own, whole, x_first, sems):
        self.here, self.own, self.whole, self.x_first = here, own, whole, x_first
        self.zs, self.zr, self.as_, self.ar, self.bs, self.br, self.local = sems
        self.kept = pltpu.make_async_copy(own, whole.at[here.z, here.x, here.y], self.local)

    @staticmethod
    def scratch(nz, ny):
        return [DMA((2, nz)), DMA((nz,)), DMA((nz, ny)), DMA((nz, ny)), DMA((nz, 2, ny)), DMA((nz, 2, ny)), DMA]

    def _along(self, source, up, own=False):
        h = self.here
        spot = self.whole.at[source, h.x, h.y]
        to = h.device(z=lax.min(h.z + 1, h.nz - 1)) if up else h.device(z=lax.max(h.z - 1, 0))
        src = self.own if own else spot
        return remote(src, spot, self.zs.at[0 if up else 1, source], self.zr.at[source], to)

    def _to_x(self, source, y, out, own=False):
        h = self.here
        spot = self.whole.at[source, h.x if out else 1 - h.x, y]
        s, r = (self.as_, self.ar) if self.x_first else (self.bs, self.br)
        i = (source, 0) if self.x_first else (source, 0, y)
        return remote(self.own if own else spot, spot, s.at[i], r.at[i], h.device(x=1 - h.x))

    def _to_y(self, source, x, e, out, own=False):
        h = self.here
        spot = self.whole.at[source, x, h.y if out else lax.rem(h.y + h.ny - e, h.ny)]
        s, r = (self.bs, self.br) if self.x_first else (self.as_, self.ar)
        i = (source, x, e) if self.x_first else (source, e)
        return remote(self.own if own else spot, spot, s.at[i], r.at[i], h.device(y=lax.rem(h.y + e, h.ny)))

    def start_z(self):
        h = self.here
        pl.when(h.z < h.nz - 1)(self._along(h.z, True, True).start)
        pl.when(h.z > 0)(self._along(h.z, False, True).start)

    def take_z(self, source, up):
        h = self.here
        self._along(source, up).wait_recv()
        pl.when(h.z < h.nz - 1 if up else h.z > 0)(self._along(source, up).start)

    def spread(self, source, own):
        h = self.here
        if self.x_first:
            self._to_x(source, h.y, True, own).start()
            for e in range(1, h.ny):
                self._to_y(source, h.x, e, True, own).start()
        else:
            for e in range(1, h.ny):
                self._to_y(source, h.x, e, True, own).start()
            self._to_x(source, h.y, True, own).start()

    def second(self, source):
        h = self.here
        if self.x_first:
            self._to_x(source, h.y, False).wait_recv()
            for e in range(1, h.ny):
                self._to_y(source, 1 - h.x, e, True).start()
        else:
            for e in range(1, h.ny):
                self._to_y(source, h.x, e, False).wait_recv()
                self._to_x(source, lax.rem(h.y + h.ny - e, h.ny), True).start()

    def third(self, source):
        h = self.here
        if self.x_first:
            for e in range(1, h.ny):
                self._to_y(source, h.x, e, False).wait_recv()
                self._to_y(source, 1 - h.x, e, False).wait_recv()
        else:
            for y in range(h.ny):
                self._to_x(source, y, False).wait_recv()

    def finish(self):
        h = self.here
        for source in range(h.nz):
            pl.when(jnp.logical_and(source <= h.z, h.z < h.nz - 1))(self._along(source, True).wait_send)
            pl.when(jnp.logical_and(source >= h.z, h.z > 0))(self._along(source, False).wait_send)
            if self.x_first:
                self._to_x(source, h.y, True).wait_send()
                for e in range(1, h.ny):
                    for x in range(2):
                        self._to_y(source, x, e, True).wait_send()
            else:
                for e in range(1, h.ny):
                    self._to_y(source, h.x, e, True).wait_send()
                for y in range(h.ny):
                    self._to_x(source, y, True).wait_send()


class GatherRows:
    def __init__(self, here, own, whole, sems):
        self.here, self.own, self.whole = here, own, whole
        self.zs, self.zr, self.xs, self.xr, self.cs, self.cr, self.local = sems
        self.kept = pltpu.make_async_copy(own, whole.at[here.z, here.x, here.core], self.local)

    @staticmethod
    def scratch(nz):
        return [DMA((2, nz)), DMA((nz,)), DMA((nz,)), DMA((nz,)), DMA((nz, 2)), DMA((nz, 2)), DMA]

    def _along(self, source, up, own=False):
        h = self.here
        spot = self.whole.at[source, h.x, h.core]
        to = h.device(z=lax.min(h.z + 1, h.nz - 1)) if up else h.device(z=lax.max(h.z - 1, 0))
        src = self.own if own else spot
        return remote(src, spot, self.zs.at[0 if up else 1, source], self.zr.at[source], to)

    def _to_x(self, source, out, own=False):
        h = self.here
        spot = self.whole.at[source, h.x if out else 1 - h.x, h.core]
        return remote(self.own if own else spot, spot, self.xs.at[source], self.xr.at[source], h.device(x=1 - h.x))

    def _to_core(self, source, x, out, own=False):
        h = self.here
        spot = self.whole.at[source, x, h.core if out else 1 - h.core]
        return remote(self.own if own else spot, spot, self.cs.at[source, x], self.cr.at[source, x], h.device(core=1 - h.core))

    start_z = Gather.start_z
    take_z = Gather.take_z

    def spread(self, source, own):
        self._to_x(source, True, own).start()
        self._to_core(source, self.here.x, True, own).start()

    def second(self, source):
        self._to_x(source, False).wait_recv()
        self._to_core(source, 1 - self.here.x, True).start()

    def third(self, source):
        for x in range(2):
            self._to_core(source, x, False).wait_recv()

    def finish(self):
        h = self.here
        for source in range(h.nz):
            pl.when(jnp.logical_and(source <= h.z, h.z < h.nz - 1))(self._along(source, True).wait_send)
            pl.when(jnp.logical_and(source >= h.z, h.z > 0))(self._along(source, False).wait_send)
            self._to_x(source, True).wait_send()
            for x in range(2):
                self._to_core(source, x, True).wait_send()


def at_distance(here, k, act):
    if k == 0:
        act(here.z, None)
    else:
        pl.when(here.z >= k)(lambda: act(here.z - k, True))
        pl.when(here.z + k < here.nz)(lambda: act(here.z + k, False))


def natural_of(shape, axis, rows_in, ny):
    lane = lax.broadcasted_iota(jnp.int32, shape, axis)
    within = lax.rem(lane, 2 * ny * rows_in)
    core = lax.rem(lax.div(within, rows_in), 2)
    y = lax.div(within, 2 * rows_in)
    return lane - within + (core * ny + y) * rows_in + lax.rem(lane, rows_in)


def bias_piece(entry, rows_in, ny):
    device = lax.div(entry, 2 * rows_in)
    chip = lax.div(device, 2 * ny)
    row = chip * 2 * ny + lax.rem(device, ny) * 2 + lax.rem(lax.div(device, ny), 2)
    return row, 6 * rows_in + lax.rem(entry, 2 * rows_in)


def greet(devices):
    barrier = pltpu.get_barrier_semaphore()
    for device in devices:
        pl.semaphore_signal(barrier, inc=1, device_id=device, device_id_type=MESH)
    return lambda: pl.semaphore_wait(barrier, len(devices))


def owner_of(chips):
    per_core = HEADS // 2
    return [int((j + 0.5) * chips / per_core) for j in range(per_core)]


def head_here(chip, slots):
    mine, has = jnp.int32(0), jnp.int32(0)
    for j, slot in enumerate(slots):
        same = (chip == slot).astype(jnp.int32)
        mine = mine + j * same
        has = has + same
    return mine, has


def attend_kernel(
    nz, ny, x_ref, mw_ref, up_ref, dn_ref,
    mw_all, up_all, dn_all, h_ref, q_ref, k_ref, v_ref, ot_ref, top_ref, att_ref, x2_ref,
    xs, wt, vc, vt_ref, o_ref, pm, x_own, up_own, dn_own, load, att_s, att_r, pass_s, pass_r, *sems,
):
    here = Here(nz, ny)
    chips = 2 * nz
    slots = owner_of(chips)
    head = q_ref.shape[1]
    width = x_ref.shape[1]
    tile = 2 * x_ref.shape[0]
    mine, has = head_here(here.chip, slots)
    odd = lax.rem(mine, 2) == 1
    rows_sems, mw_sems, up_sems, dn_sems = sems[:7], sems[7:14], sems[14:21], sems[21:28]

    peers = [here.device(z=here.after(d)) for d in range(1, nz)]
    peers += [here.device(x=1 - here.x), here.device(core=1 - here.core)]
    peers += [here.device(z=here.after(d), x=1 - here.x) for d in range(1, nz)]
    peers += [here.device(y=lax.rem(here.y + e, ny)) for e in range(1, ny)]
    met = greet(peers)
    half = width // 2
    unit = up_ref.shape[1]
    rows_in = unit // 2
    pair_rows = HEADS // 4 * unit
    from_row = lax.broadcasted_iota(jnp.int32, (width, width), 0)
    pm[...] = (from_row == natural_of((1, width), 1, rows_in, ny)).astype(LOW)
    x_own[...] = dot(x_ref[...], pm[...], (1, 0)).astype(LOW)
    dn_own[...] = dot(dn_ref[...], pm[...], (1, 0)).astype(LOW)
    up_own[...] = up_ref[...]
    up_own[4] = dot(up_ref[4], pm[:half, :half], (1, 0)).astype(LOW)
    rows = GatherRows(here, x_own, xs, rows_sems)
    mw = Gather(here, mw_ref, mw_all, True, mw_sems)
    up = Gather(here, up_own, up_all, True, up_sems)
    dn = Gather(here, dn_own, dn_all, False, dn_sems)
    first, later = (rows, mw), (up, dn)
    for item in first + later:
        item.kept.start()
    met()

    def take(items, k):
        def act(source, way):
            for item in items:
                if k:
                    item.take_z(source, way)
            for item in items:
                item.spread(source, k == 0)

        at_distance(here, k, act)

    def then(items, k, stage):
        def act(source, _):
            for item in items:
                getattr(item, stage)(source)

        at_distance(here, k, act)

    for item in first:
        item.start_z()
    take(first, 0)
    for k in range(1, nz):
        take(first, k)
        then(first, k - 1, "second")
    for item in later:
        item.start_z()
    then(first, nz - 1, "second")
    take(later, 0)
    for k in range(nz):
        then((mw,), k, "third")
    mw.kept.wait()
    my_pair = pl.ds(pl.multiple_of(lax.div(mine, 2) * unit, unit), unit)
    pair = pltpu.make_async_copy(mw_all.at[:, :, :, my_pair], wt, load.at[0])
    pair.start()
    vectors = pltpu.make_async_copy(mw_all.at[:, :, :, pl.ds(pair_rows, 16)], vc, load.at[1])
    vectors.start()
    for k in range(nz):
        then((rows,), k, "third")
    rows.kept.wait()
    pair.wait()
    vectors.wait()
    keep_rows = pltpu.make_async_copy(xs.at[here.z, here.x], x2_ref, load.at[2])
    keep_rows.start()

    steps = []
    for k in range(1, nz):
        steps += [partial(take, later, k), partial(then, later, k - 1, "second")]
    steps += [partial(then, later, nz - 1, "second")] + [partial(then, later, k, "third") for k in range(nz)]

    @pl.when(has == 1)
    def _():
        pieces = vc[...].reshape(-1, vc.shape[-1])
        count = 2 * chips * ny
        pick_row = lax.broadcasted_iota(jnp.int32, (count, pieces.shape[0]), 0) * 8
        pick = (pick_row == lax.broadcasted_iota(jnp.int32, pick_row.shape, 1)).astype(LOW)
        pieces = dot(pick, pieces, (1, 0)).astype(LOW)
        lane = lax.broadcasted_iota(jnp.int32, (1, width), 1)
        pair_lane = lax.broadcasted_iota(jnp.int32, (1, 2 * head), 1)
        pair_lane = pair_lane + (here.core * (HEADS // 4) + lax.div(mine, 2)) * 2 * head
        q_row, q_col = bias_piece(pair_lane, rows_in, ny)
        v_row, v_col = bias_piece(pair_lane + width, rows_in, ny)
        none = jnp.full((1, 2 * head), -1, jnp.int32)
        in_row, owner = lax.rem(lane, rows_in), lax.div(lane, rows_in)
        cols = jnp.concatenate([in_row, rows_in + in_row, q_col, none, v_col], axis=1)
        owners = jnp.concatenate([owner, owner, q_row, none, v_row], axis=1)
        spot = lax.broadcasted_iota(jnp.int32, (pieces.shape[1], cols.shape[1]), 0)
        moved = dot(pieces, (spot == cols).astype(LOW), (1, 0))
        from_row = lax.broadcasted_iota(jnp.int32, moved.shape, 0)
        flat = jnp.sum(jnp.where(from_row == owners, moved, 0.0), axis=0, keepdims=True)
        gain, shift, bias = flat[:, :width], flat[:, width : 2 * width], flat[:, 2 * width :]
        weight = wt[...].reshape(width, -1)

        def choose(values):
            return jnp.where(odd, values[:, head:], values[:, :head])

        for i in range(chips):
            span = slice(i * tile, (i + 1) * tile)
            values = xs[i // 2, i % 2].reshape(tile, width).astype(FULL)
            normed, _ = normalize(values)
            low = (normed * gain + shift).astype(LOW)
            h_ref[span, :] = low
            mixed = (dot(low, weight, (1, 0)) + bias).astype(LOW)
            q_ref[span, :] = (choose(mixed[:, : 2 * head]) * (head ** (-0.5))).astype(LOW)
            k_ref[span, :] = choose(mixed[:, 2 * head : 4 * head])
            value = choose(mixed[:, 4 * head :])
            v_ref[span, :] = value
            vt_ref[:, span] = value.T

    def query_tile(i):
        span = slice(i * tile, (i + 1) * tile)
        query = q_ref[span, :]

        def absorb(j, carry, masked):
            top, total, acc = carry
            keys = slice(j * tile, (j + 1) * tile)
            scores = dot(k_ref[keys, :], query, (1, 1))
            if masked:
                key_pos = lax.broadcasted_iota(jnp.int32, scores.shape, 0)
                query_pos = lax.broadcasted_iota(jnp.int32, scores.shape, 1)
                scores = jnp.where(key_pos <= query_pos, scores, NEGATIVE)
            new_top = jnp.maximum(top, jnp.max(scores, axis=0, keepdims=True))
            weights = jnp.exp(scores - new_top)
            keep = jnp.exp(top - new_top)
            total = total * keep + jnp.sum(weights, axis=0, keepdims=True)
            acc = acc * keep + dot(vt_ref[:, keys], weights.astype(LOW), (1, 0))
            return new_top, total, acc

        carry = (jnp.full((1, tile), NEGATIVE, FULL), jnp.zeros((1, tile), FULL), jnp.zeros((head, tile), FULL))
        for j in range(i + 1):
            carry = absorb(j, carry, j == i)
        top, total, acc = carry
        out = acc / total
        ot_ref[:, span] = out
        o_ref[i] = out.T.astype(LOW)
        top_ref[:, span] = top + jnp.log(total)

    def hand(i):
        spot = att_ref.at[here.core, mine]
        return (
            pltpu.make_async_copy(o_ref.at[i], spot, att_s.at[i]),
            remote(o_ref.at[i], spot, att_s.at[i], att_r.at[mine], here.device(z=i // 2, x=i % 2)),
        )

    for i in range(chips):
        @pl.when(has == 1)
        def _(i=i):
            query_tile(i)
            stay, leave = hand(i)
            pl.when(here.chip == i)(stay.start)
            pl.when(here.chip != i)(leave.start)

        if i < len(steps):
            steps[i]()
    for step in steps[chips:]:
        step()

    for i in range(chips):
        @pl.when(has == 1)
        def _(i=i):
            stay, leave = hand(i)
            pl.when(here.chip == i)(stay.wait)
            pl.when(here.chip != i)(leave.wait_send)

    for j, slot in enumerate(slots):
        @pl.when(here.chip != slot)
        def _(j=j, slot=slot):
            spot = att_ref.at[here.core, j]
            remote(spot, spot, att_s.at[0], att_r.at[j], here.device(z=slot // 2, x=slot % 2)).wait_recv()

    spot = att_ref.at[here.core]
    give = remote(spot, spot, pass_s, pass_r, here.device(core=1 - here.core))
    give.start()
    spot = att_ref.at[1 - here.core]
    remote(spot, spot, pass_s, pass_r, here.device(core=1 - here.core)).wait_recv()
    give.wait_send()
    keep_rows.wait()
    for item in later:
        item.kept.wait()
    for item in first + later:
        item.finish()


def attend(nz, ny, own, mw, up, dn):
    span, width = own.shape
    length = 4 * nz * span
    head = width // HEADS
    units = (nz, 2, ny)
    low = jax.ShapeDtypeStruct((length, head), LOW)
    anywhere = pl.BlockSpec(memory_space=pl.ANY)
    vmem = pl.BlockSpec(memory_space=pltpu.VMEM)
    return pl.pallas_call(
        partial(attend_kernel, nz, ny),
        out_shape=(
            jax.ShapeDtypeStruct(units + mw.shape, LOW),
            jax.ShapeDtypeStruct(units + up.shape, LOW),
            jax.ShapeDtypeStruct(units + dn.shape, LOW),
            jax.ShapeDtypeStruct((length, width), LOW),
            low,
            low,
            low,
            jax.ShapeDtypeStruct((head, length), FULL),
            jax.ShapeDtypeStruct((1, length), FULL),
            jax.ShapeDtypeStruct((2, HEADS // 2, 2 * span, head), LOW),
            jax.ShapeDtypeStruct((2, span, width), LOW),
        ),
        in_specs=[vmem] * 4,
        out_specs=[anywhere] * 3 + [vmem] * 6 + [anywhere] * 2,
        scratch_shapes=[
            pltpu.VMEM((nz, 2, 2, span, width), LOW),
            pltpu.VMEM(units + up.shape[1:], LOW),
            pltpu.VMEM(units + (16,) + mw.shape[1:], LOW),
            pltpu.VMEM((head, length), LOW),
            pltpu.VMEM((2 * nz, 2 * span, head), LOW),
            pltpu.VMEM((width, width), LOW),
            pltpu.VMEM(own.shape, LOW),
            pltpu.VMEM(up.shape, LOW),
            pltpu.VMEM(dn.shape, LOW),
            DMA((3,)),
            DMA((2 * nz,)),
            DMA((HEADS // 2,)),
            DMA,
            DMA,
        ]
        + GatherRows.scratch(nz)
        + Gather.scratch(nz, ny) * 3,
        compiler_params=pltpu.CompilerParams(vmem_limit_bytes=56 << 20, collective_id=0, has_side_effects=True),
        cost_estimate=pl.CostEstimate(
            flops=6 * length * length * head, bytes_accessed=8 * length * width, transcendentals=length * length
        ),
        name="attend",
    )(own, mw, up, dn)


GELU_K = 0.7978845608028654
GELU_C = 0.044715


def gelu_pair(u):
    square = u * u
    tanh = jnp.tanh(GELU_K * u * (1.0 + GELU_C * square))
    half = 0.5 * (1.0 + tanh)
    slope = half + (0.5 * GELU_K) * u * (1.0 - tanh * tanh) * (1.0 + 3.0 * GELU_C * square)
    return u * half, slope


def split_dot(values, turn, dims):
    high = values.astype(LOW)
    rest = values - high.astype(FULL)
    middle = rest.astype(LOW)
    low = (rest - middle.astype(FULL)).astype(LOW)
    return dot(high, turn, dims) + dot(middle, turn, dims) + dot(low, turn, dims)


def rest_kernel(
    nz, hidden_tile,
    x2_ref, att_ref, cot_ref, mw_all, up_ref, dn_ref,
    q_ref, k_ref, v_ref, ot_ref, top_ref, h_all,
    act_ref, ing_ref, fin, swap, mixf, mix_swap, vec_ref,
    up, dn, ow, own, pm, vc, att, cot, h2, act_low, gu, branch, feed, feed_in, gh2, gh2_in, gmid, eb, grads, go_send,
    go_all, kt_ref, got_ref, delta_ref, gqt_ref, gsend, gat, mw, hbuf, head_acc, head_sum, hs_in, mix_in,
    r1, r2, r3, pack, vec_in,
    load, near_s, near_r, h_s, go_s, go_r, kv_s, kv_r, q_s, q_r, s1, t1, s2, t2, s3, t3, ex_s, ex_r,
    vec_s, vec_r, mix_s, mix_r,
):
    ny = 2
    here = Here(nz, ny)
    core, chip, x, y, z = here.core, here.chip, here.x, here.y, here.z
    chips = 2 * nz
    parts = 4 * nz * ny
    slots = owner_of(chips)
    per_core = len(slots)
    length, head = q_ref.shape
    tile = length // chips
    _, span, width = cot_ref.shape
    half = width // 2
    hidden = dn_ref.shape[0]
    rows_hid = 2 * hidden // parts
    factor = head ** (-0.5)
    job, has = head_here(chip, slots)
    partner = here.device(core=1 - core)
    slabs, unit = grads.shape[4], grads.shape[5]
    pairs = per_core // 2
    rows_in = unit // 2
    my_rows = pl.ds(pl.multiple_of(core * span, span), span)
    their_rows = pl.ds(pl.multiple_of((1 - core) * span, span), span)

    def flat(zz, xx, yy, cc):
        return ((zz * 2 + xx) * ny + yy) * 2 + cc

    others = []
    for dz in range(nz):
        for dx in range(2):
            for dy in range(ny):
                for dc in range(2):
                    if dz or dx or dy or dc:
                        zz = lax.rem(z + dz, nz)
                        xx = 1 - x if dx else x
                        yy = 1 - y if dy else y
                        cc = 1 - core if dc else core
                        behind = (lax.rem(z + nz - dz, nz), xx, yy, cc)
                        others.append((here.device(zz, xx, cc, yy), flat(zz, xx, yy, cc), flat(*behind)))

    loads = [
        pltpu.make_async_copy(up_ref.at[:, :, :, 4], ow.at[core], load.at[0]),
        pltpu.make_async_copy(mw_all.at[:, :, :, pl.ds(pairs * unit, 16)], vc, load.at[1]),
        pltpu.make_async_copy(dn_ref, dn, load.at[2]),
        pltpu.make_async_copy(mw_all.at[:, :, :, pl.ds(0, pairs * unit)], mw, load.at[3]),
    ]
    for t in range(4):
        spot = up.at[:, :, :, :, pl.ds(t * half, half)]
        loads.append(pltpu.make_async_copy(up_ref.at[:, :, :, t], spot, load.at[4 + t]))
    for copy in loads:
        copy.start()
    met = greet([device for device, _, _ in others])

    def pass_on(i, src, dst):
        return remote(src, dst, near_s.at[i], near_r.at[i], partner)

    natural = natural_of((1, width), 1, rows_in, ny)
    from_row = lax.broadcasted_iota(jnp.int32, (width, width), 0)
    pm[...] = (from_row == natural).astype(LOW)
    for d in range(2):
        cot[d, my_rows, :] = dot(cot_ref[d], pm[...], (1, 0)).astype(LOW)
    met()
    give_cot = pass_on(0, cot.at[:, my_rows], cot.at[:, my_rows])
    give_cot.start()
    loads[0].wait()
    give_ow = pass_on(1, ow.at[core], ow.at[core])
    give_ow.start()

    wide = lax.broadcasted_iota(jnp.int32, (1, width), 1)
    wide_owner = lax.div(wide, rows_in)
    hid = lax.broadcasted_iota(jnp.int32, (1, hidden), 1)
    hid_owner = lax.div(hid, rows_hid) * 2 + core
    in_row = lax.rem(wide, rows_in)
    cols = [in_row + i * rows_in for i in (2, 3, 4, 5, 0)] + [lax.rem(hid, rows_hid) + 8 * rows_in]
    cols = jnp.concatenate(cols, axis=1)
    owners = jnp.concatenate([wide_owner] * 5 + [hid_owner], axis=1)
    loads[1].wait()
    pieces = vc[...].reshape(-1, vc.shape[-1])
    pick_row = lax.broadcasted_iota(jnp.int32, (parts, pieces.shape[0]), 0) * 8
    pick = (pick_row == lax.broadcasted_iota(jnp.int32, pick_row.shape, 1)).astype(LOW)
    pieces = dot(pick, pieces, (1, 0)).astype(LOW)
    spot = lax.broadcasted_iota(jnp.int32, (pieces.shape[1], cols.shape[1]), 0)
    moved = dot(pieces, (spot == cols).astype(LOW), (1, 0))
    piece_row = lax.broadcasted_iota(jnp.int32, moved.shape, 0)
    vectors = jnp.sum(jnp.where(piece_row == owners, moved, 0.0), axis=0, keepdims=True)
    gain, shift, out_bias, down_bias, first_gain = (vectors[:, i * width : (i + 1) * width] for i in range(5))
    up_bias = vectors[:, 5 * width :]

    natural_att = jnp.concatenate([att_ref[c, j] for c in range(2) for j in range(per_core)], axis=1)
    att[...] = dot(natural_att, pm[...], (1, 0)).astype(LOW)
    remote(ow.at[1 - core], ow.at[1 - core], near_s.at[1], near_r.at[1], partner).wait_recv()
    for c in range(2):
        own[:, c * half : (c + 1) * half] = dot(pm[...], ow[c].reshape(width, half), (1, 0)).astype(LOW)
    branch[...] = dot(natural_att, own[...], (1, 0)) + out_bias

    def middle_of(d, rows):
        return x2_ref[rows, :].astype(FULL) + SCALES[d] * branch[rows, :]

    for d in range(2):
        n, _ = normalize(middle_of(d, slice(None)))
        h2[d] = (n * gain + shift).astype(LOW)
    theirs_cot = cot.at[:, their_rows]
    remote(theirs_cot, theirs_cot, near_s.at[0], near_r.at[0], partner).wait_recv()
    loads[2].wait()
    for copy in loads[4:]:
        copy.wait()

    def up_cols(cut):
        return up[:, :, :, :, cut].reshape(width, -1)

    def upstream(d):
        return (SCALES[d] * cot[d].astype(FULL)).astype(LOW)

    stride = pack.shape[1] * pack.shape[2] // 2
    lane = lax.broadcasted_iota(jnp.int32, (width, 128), 0)
    in_piece = (lax.rem(lane, rows_in) == lax.broadcasted_iota(jnp.int32, lane.shape, 1)).astype(LOW)

    def placed(vector, owner, turn, start):
        rows = lax.broadcasted_iota(jnp.int32, (parts, vector.shape[1]), 0)
        spread = jnp.where(rows == owner, vector, 0.0)
        high = spread.astype(LOW)
        low = (spread - high.astype(FULL)).astype(LOW)
        values = dot(high, turn, (1, 0)) + dot(low, turn, (1, 0))
        return jnp.pad(values, ((0, 0), (start, 2 * stride)))[:, : 2 * stride]

    sums = {}

    def row_sum(v, d, values):
        sums[v, d] = jnp.sum(values, axis=0, keepdims=True)

    exchanges = []

    def forth(d):
        low_in = upstream(d)
        ups = []
        for t in range(0, hidden, hidden_tile):
            cut = slice(t, t + hidden_tile)
            u = dot(h2[d], up_cols(cut), (1, 0)) + up_bias[:, cut]
            active, slope = gelu_pair(u)
            active = active.astype(LOW)
            act_low[d, :, cut] = active
            grad = (dot(low_in, dn[cut, :], (1, 1)) * slope).astype(LOW)
            gu[d, :, cut] = grad
            ups.append(jnp.sum(grad.astype(FULL), axis=0, keepdims=True))
        sums["up", d] = jnp.concatenate(ups, axis=1)

    def back_to_width(d):
        gh2[d] = dot(gu[d], up_cols(slice(None)), (1, 1))
        feed[d] = dot(act_low[d], dn[...], (1, 0))
        for i, (src, dst) in ((2, (gh2, gh2_in)), (4, (feed, feed_in))):
            copy = pass_on(i + d, src.at[d, their_rows], dst.at[d])
            copy.start()
            exchanges.append(copy)

    def keep(d, values, first_row, first_col, base, rows_of):
        for i in range(0, values.shape[0], unit):
            row = first_row + i
            u, within = row // rows_of, (row % rows_of) // unit
            place = (u // (2 * ny), (u // ny) % 2, u % ny)
            for c in range(0, values.shape[1], half):
                slab = base + within * 2 + (first_col + c) // half
                grads[(d,) + place + (slab,)] = values[i : i + unit, c : c + half]

    def down_grads(d):
        low_in = upstream(d)
        for t in range(0, hidden, half):
            keep(d, dot(act_low[d, :, t : t + half], low_in, (0, 0)).astype(LOW), t, 0, 0, 2 * unit)

    def up_grads(d):
        for t in range(0, hidden, 2 * half):
            for m in range(0, width, half):
                part = dot(h2[d, :, m : m + half], gu[d, :, t : t + 2 * half], (0, 0)).astype(LOW)
                keep(d, part, m, t, 4, unit)

    def norm_feed_back(d):
        remote(gh2_in.at[d], gh2_in.at[d], near_s.at[2 + d], near_r.at[2 + d], partner).wait_recv()
        grad = gh2[d, my_rows, :] + gh2_in[d]
        n, r = normalize(middle_of(d, my_rows))
        row_sum(2, d, grad * n)
        row_sum(3, d, grad)
        own_cot = cot[d, my_rows, :].astype(FULL)
        middle_grad = own_cot + norm_back(grad, n, r, gain)
        gmid[d] = middle_grad
        branch_low = (SCALES[d] * middle_grad).astype(LOW)
        row_sum(4, d, branch_low.astype(FULL))
        row_sum(5, d, (SCALES[d] * own_cot).astype(LOW).astype(FULL))
        eb[d, my_rows, :] = branch_low
        copy = pass_on(6 + d, eb.at[d, my_rows], eb.at[d, my_rows])
        copy.start()
        exchanges.append(copy)

    zis = []
    for i in range((nz + 1) // 2):
        zis += [nz - 1 - i] + ([i] if i != nz - 1 - i else [])
    cuts = [(0, slabs // 2), (slabs // 2, slabs)]
    chunks = [(zi, part) for part in range(len(cuts)) for zi in zis]

    def y_first(d, zi, part):
        return d == 0 or chunks.index((zi, part)) % 2 == 1

    def mine(d, zi, part, i, slab):
        return grads.at[d, zi, i, y, slab] if y_first(d, zi, part) else grads.at[d, zi, x, i, slab]

    def some(part):
        return pl.ds(cuts[part][0], cuts[part][1] - cuts[part][0])

    def stage1(d, zi, part):
        slab = some(part)
        if y_first(d, zi, part):
            src, to = grads.at[d, zi, :, 1 - y, slab], here.device(y=1 - y)
        else:
            src, to = grads.at[d, zi, 1 - x, :, slab], here.device(x=1 - x)
        return remote(src, r1.at[d, zi, :, slab], s1.at[d, zi, part], t1.at[d, zi, part], to)

    def stage2(d, zi, part):
        slab = some(part)
        if y_first(d, zi, part):
            src, to = mine(d, zi, part, 1 - x, slab), here.device(x=1 - x)
        else:
            src, to = mine(d, zi, part, 1 - y, slab), here.device(y=1 - y)
        return remote(src, r2.at[d, zi, slab], s2.at[d, zi, part], t2.at[d, zi, part], to)

    def spare(zi, up):
        return zi if up else jnp.where(z - 1 == zi, nz, zi)

    def stage3(d, zi, part, up):
        to = here.device(z=lax.min(z + 1, nz - 1)) if up else here.device(z=lax.max(z - 1, 0))
        way = 0 if up else 1
        slab = some(part)
        src, dst = r2.at[d, zi, slab], r3.at[d, spare(zi, up), slab]
        return remote(src, dst, s3.at[d, zi, part], t3.at[d, way, zi, part], to)

    def arrive3(d, zi, part, up):
        way = 0 if up else 1
        spot = r3.at[d, zi, some(part)]
        return remote(spot, spot, s3.at[d, zi, part], t3.at[d, way, zi, part], partner)

    def begin(d, n):
        if n < len(chunks):
            stage1(d, *chunks[n]).start()

    def add_into(target, other, lead):
        def one(i, _):
            a, b = target(i), other(i)
            a[...] = (a[...].astype(FULL) + b[...].astype(FULL)).astype(LOW)
            return 0

        lax.fori_loop(0, lead, one, 0)

    def after1(d, zi, part):
        stage1(d, zi, part).wait_recv()
        low, high = cuts[part]
        size = high - low
        add_into(
            lambda i: mine(d, zi, part, lax.div(i, size), low + lax.rem(i, size)),
            lambda i: r1.at[d, zi, lax.div(i, size), low + lax.rem(i, size)],
            2 * size,
        )
        stage2(d, zi, part).start()

    def after2(d, zi, part):
        low, high = cuts[part]
        stage2(d, zi, part).wait_recv()
        own_place = x if y_first(d, zi, part) else y
        add_into(lambda i: r2.at[d, zi, low + i], lambda i: mine(d, zi, part, own_place, low + i), high - low)
        if zi > 0:
            pl.when(z == 0)(stage3(d, zi, part, True).start)
        if zi < nz - 1:
            pl.when(z == nz - 1)(stage3(d, zi, part, False).start)

    def after3(d, zi, part, far):
        low, high = cuts[part]
        if far < zi:
            @pl.when(z == far)
            def _():
                arrive3(d, zi, part, True).wait_recv()
                add_into(lambda i: r2.at[d, zi, low + i], lambda i: r3.at[d, zi, low + i], high - low)
                stage3(d, zi, part, True).start()

        if nz - 1 - far > zi:
            @pl.when(z == nz - 1 - far)
            def _():
                arrive3(d, zi, part, False).wait_recv()
                add_into(lambda i: r2.at[d, zi, low + i], lambda i: r3.at[d, zi, low + i], high - low)
                stage3(d, zi, part, False).start()

    def last3(d, zi, part):
        low, high = cuts[part]

        @pl.when(z == zi)
        def _():
            if zi > 0:
                arrive3(d, zi, part, True).wait_recv()
            if zi < nz - 1:
                arrive3(d, zi, part, False).wait_recv()

            def one(i, _):
                total = r2[d, zi, i].astype(FULL)
                if zi > 0:
                    total = total + r3[d, zi, i].astype(FULL)
                if zi < nz - 1:
                    total = total + r3[d, nz, i].astype(FULL)
                fin[d, i] = total
                return 0

            lax.fori_loop(low, high, one, 0)

    def advance(n):
        stages = [after1, after2] + [partial(after3, far=far) for far in range(1, nz - 1)] + [last3]
        for behind, stage in enumerate(stages):
            for d in range(2):
                if 0 <= n - behind < len(chunks):
                    stage(d, *chunks[n - behind])
                if not behind:
                    begin(d, n + 2)

    steps = len(chunks) + nz

    def finish_sends():
        for zi, part in chunks:
            for d in range(2):
                stage1(d, zi, part).wait_send()
                stage2(d, zi, part).wait_send()
                pl.when(z != zi)(stage3(d, zi, part, True).wait_send)

    for d in range(2):
        forth(d)
        down_grads(d)
        begin(d, 0)
        begin(d, 1)
    for d in range(2):
        back_to_width(d)
    up_grads(0)
    norm_feed_back(0)
    up_grads(1)
    norm_feed_back(1)

    def go_copies(j):
        slot = slots[j]
        return (
            pltpu.make_async_copy(go_send.at[j], go_all.at[chip], go_s.at[j]),
            remote(go_send.at[j], go_all.at[chip], go_s.at[j], go_r.at[chip], here.device(z=slot // 2, x=slot % 2)),
        )

    own_half = own.at[pl.ds(pl.multiple_of(core * half, half), half), :]
    for d in range(2):
        spot = eb.at[d, their_rows]
        remote(spot, spot, near_s.at[6 + d], near_r.at[6 + d], partner).wait_recv()
        go = dot(eb[d], own_half[...], (1, 1)).astype(LOW)
        for j in range(per_core):
            go_send[j, :, d * head : (d + 1) * head] = go[:, j * head : (j + 1) * head]
    for j, slot in enumerate(slots):
        stay, leave = go_copies(j)
        pl.when(chip == slot)(stay.start)
        pl.when(chip != slot)(leave.start)
    for d in range(2):
        ours = eb[d, :, pl.ds(pl.multiple_of(core * half, half), half)]
        for m in range(0, width, half):
            keep(d, dot(att[:, m : m + half], ours, (0, 0)).astype(LOW), m, 0, 8, unit)

    for d in range(2):
        remote(feed_in.at[d], feed_in.at[d], near_s.at[4 + d], near_r.at[4 + d], partner).wait_recv()
        out = middle_of(d, my_rows) + SCALES[d] * (feed[d, my_rows, :] + feed_in[d] + down_bias)
        act_ref[d] = out.astype(LOW)
    total = jnp.zeros((parts, 2 * stride), FULL)
    for v in range(2, 6):
        for d in range(2):
            total = total + placed(sums[v, d], wide_owner, in_piece, v * rows_in + d * stride)
    hid_lane = lax.broadcasted_iota(jnp.int32, (hidden, 128), 0)
    in_hidden = (lax.rem(hid_lane, rows_hid) == lax.broadcasted_iota(jnp.int32, hid_lane.shape, 1)).astype(LOW)
    for d in range(2):
        total = total + placed(sums["up", d], hid_owner, in_hidden, 8 * rows_in + d * stride)
    for c in range(pack.shape[1]):
        pack[:, c, :] = total[:, c * 128 : (c + 1) * 128]
    advance(0)

    def h_copy(i):
        rows = slice(i * tile, (i + 1) * tile)
        return pltpu.make_async_copy(h_all.at[rows], hbuf.at[i % 2], h_s.at[i % 2])

    @pl.when(has == 1)
    def _():
        h_copy(0).start()
        h_copy(1).start()
        for t in range(chips):
            stay = pltpu.make_async_copy(go_send.at[0], go_all.at[t], go_s.at[job])
            come = remote(go_send.at[0], go_all.at[t], go_s.at[0], go_r.at[t], here.device(z=t // 2, x=t % 2))
            pl.when(chip == t)(stay.wait)
            pl.when(chip != t)(come.wait_recv)
        for i in range(chips):
            rows = slice(i * tile, (i + 1) * tile)
            kt_ref[:, rows] = k_ref[rows, :].T
            up_t = go_all[i].T
            for d in range(2):
                part = up_t[d * head : (d + 1) * head, :]
                got_ref[d, :, rows] = part
                delta_ref[d, :, rows] = jnp.sum(part.astype(FULL) * ot_ref[:, rows], axis=0, keepdims=True)
                gqt_ref[d, :, rows] = jnp.zeros((head, tile), FULL)

    def key_tile(j):
        keys = slice(j * tile, (j + 1) * tile)
        key = k_ref[keys, :]
        value = v_ref[keys, :]
        key_t = kt_ref[:, keys]

        def step(i, carry, masked):
            gv, gk0, gk1 = carry
            rows = pl.ds(i * tile if masked else pl.multiple_of(i * tile, tile), tile)
            query = q_ref[rows, :]
            scores = dot(key, query, (1, 1))
            if masked:
                key_pos = lax.broadcasted_iota(jnp.int32, scores.shape, 0)
                query_pos = lax.broadcasted_iota(jnp.int32, scores.shape, 1)
                scores = jnp.where(key_pos <= query_pos, scores, NEGATIVE)
            probs = jnp.exp(scores - top_ref[:, rows])
            gv = gv + dot(probs.astype(LOW), go_all[i], (1, 0))
            gks = [gk0, gk1]
            for d in range(2):
                prob_grad = dot(value, got_ref[d, :, rows], (1, 0))
                score_low = (probs * (prob_grad - delta_ref[d, :, rows])).astype(LOW)
                gks[d] = gks[d] + dot(score_low, query, (1, 0))
                gqt_ref[d, :, rows] += dot(key_t, score_low, (1, 0))
            return gv, gks[0], gks[1]

        zero = jnp.zeros((tile, head), FULL)
        carry = step(j, (jnp.zeros((tile, 2 * head), FULL), zero, zero), True)
        gv, gk0, gk1 = lax.fori_loop(j + 1, chips, lambda i, c: step(i, c, False), carry)
        gsend[j, 1] = jnp.concatenate([gk0, gk1], axis=1).astype(LOW)
        gsend[j, 2] = gv.astype(LOW)

    def kv_copies(t):
        src, dst = gsend.at[t, pl.ds(1, 2)], gat.at[job, pl.ds(1, 2)]
        to = here.device(z=t // 2, x=t % 2)
        return pltpu.make_async_copy(src, dst, kv_s.at[t]), remote(src, dst, kv_s.at[t], kv_r.at[job], to)

    def q_copies(t):
        src, dst = gsend.at[t, 0], gat.at[job, 0]
        to = here.device(z=t // 2, x=t % 2)
        return pltpu.make_async_copy(src, dst, q_s.at[t]), remote(src, dst, q_s.at[t], q_r.at[job], to)

    def launch(copies, t):
        stay, leave = copies(t)
        pl.when(chip == t)(stay.start)
        pl.when(chip != t)(leave.start)

    between = {1: 1, 3: 2, 7: 3}
    for j in range(chips):
        @pl.when(has == 1)
        def _(j=j):
            key_tile(j)
            launch(kv_copies, j)

        if j in between:
            advance(between[j])

    @pl.when(has == 1)
    def _():
        for i in range(chips):
            rows = slice(i * tile, (i + 1) * tile)
            both = jnp.concatenate([gqt_ref[0, :, rows], gqt_ref[1, :, rows]], axis=0) * factor
            gsend[i, 0] = both.T.astype(LOW)
            launch(q_copies, i)

    def mix_y():
        return remote(head_sum.at[:, :, 1 - y], hs_in, ex_s.at[0], ex_r.at[0], here.device(y=1 - y))

    def mix_copies(t):
        src, dst = head_sum.at[t // 2, t % 2, y], mix_in.at[job]
        to = here.device(z=t // 2, x=t % 2)
        return pltpu.make_async_copy(src, dst, mix_s.at[t]), remote(src, dst, mix_s.at[t], mix_r.at[job], to)

    @pl.when(has == 1)
    def _():
        for i in range(chips):
            h_copy(i).wait()
            right = jnp.concatenate([gsend[i, t] for t in range(3)], axis=1)
            part = dot(hbuf[i % 2], right, (0, 0))
            if i == 0:
                head_acc[...] = part
            else:
                head_acc[...] += part
            if i + 2 < chips:
                h_copy(i + 2).start()
        for u in range(parts // 2):
            zz, xx, yy = u // (2 * ny), (u // ny) % 2, u % ny
            head_sum[zz, xx, yy] = head_acc[u * unit : (u + 1) * unit, :].astype(LOW)
        mix_y().start()

    advance(4)

    @pl.when(has == 1)
    def _():
        mix_y().wait_recv()
        mix_y().wait_send()
        add_into(
            lambda i: head_sum.at[lax.div(i, 2), lax.rem(i, 2), y],
            lambda i: hs_in.at[lax.div(i, 2), lax.rem(i, 2)],
            chips,
        )
        for t in range(chips):
            launch(mix_copies, t)

    biases = []
    for t in (0, 2):
        acc = jnp.zeros((1, 2 * head), FULL)
        for i in range(chips):
            acc = acc + jnp.sum(gsend[i, t].astype(FULL), axis=0, keepdims=True)
        biases.append(jnp.where(has == 1, acc, 0.0))
    total = jnp.concatenate([pack[:, c, :] for c in range(pack.shape[1])], axis=1)
    for b in range(2):
        rows = lax.broadcasted_iota(jnp.int32, (parts, 2 * head), 0)
        first_entry = (core * per_core + job) * head + b * width
        across = lax.broadcasted_iota(jnp.int32, (1, 2 * head), 1)
        down_lane = lax.broadcasted_iota(jnp.int32, (2 * head, 1), 0)
        owner, _ = bias_piece(lax.rem(across, head) + first_entry, rows_in, ny)
        _, column = bias_piece(lax.rem(down_lane, head) + first_entry, rows_in, ny)
        column = column + lax.div(down_lane, head) * stride
        spread = jnp.where(rows == owner, biases[b], 0.0)
        turn = lax.broadcasted_iota(jnp.int32, (2 * head, 2 * stride), 1) == column
        high = spread.astype(LOW)
        low = (spread - high.astype(FULL)).astype(LOW)
        total = total + dot(high, turn.astype(LOW), (1, 0)) + dot(low, turn.astype(LOW), (1, 0))
    advance(5)

    for copy in exchanges:
        copy.wait_send()
    loads[3].wait()
    for j, slot in enumerate(slots):
        @pl.when(chip != slot)
        def _(j=j, slot=slot):
            to = here.device(z=slot // 2, x=slot % 2)
            remote(gat.at[j, pl.ds(1, 2)], gat.at[j, pl.ds(1, 2)], kv_s.at[0], kv_r.at[j], to).wait_recv()
            remote(gat.at[j, 0], gat.at[j, 0], q_s.at[0], q_r.at[j], to).wait_recv()

        @pl.when(chip == slot)
        def _(j=j, slot=slot):
            kv_copies(slot)[0].wait()
            q_copies(slot)[0].wait()

    def first_swap(d):
        return remote(gh2.at[d, their_rows], gh2_in.at[d], ex_s.at[1 + d], ex_r.at[1 + d], partner)

    for d in range(2):
        lanes = slice(d * head, (d + 1) * head)
        first = None
        for p in range(per_core // 2):
            left = jnp.concatenate(
                [gat[2 * p + o, t][:, lanes] for t in range(3) for o in range(2)], axis=1
            )
            part = dot(left, mw[:, :, :, p * unit : (p + 1) * unit].reshape(width, half), (1, 1))
            first = part if first is None else first + part
        gh2[d] = first
        first_swap(d).start()
    normed, inv = normalize(x2_ref[my_rows, :].astype(FULL))
    for d in range(2):
        first_swap(d).wait_recv()
        grad = gh2[d, my_rows, :] + gh2_in[d]
        for v, row in ((0, jnp.sum(grad * normed, axis=0, keepdims=True)), (1, jnp.sum(grad, axis=0, keepdims=True))):
            total = total + placed(row, wide_owner, in_piece, v * rows_in + d * stride)
        whole = gmid[d] + norm_back(grad, normed, inv, first_gain)
        ing_ref[d] = whole
    for c in range(pack.shape[1]):
        pack[:, c, :] = total[:, c * 128 : (c + 1) * 128]
    me = flat(z, x, y, core)

    def vec_copy(n):
        device, index, _ = others[n]
        return remote(pack.at[index], vec_in.at[me], vec_s.at[n], vec_r.at[n], device)

    def vec_come(n):
        device, _, index = others[n]
        return remote(pack.at[index], vec_in.at[index], vec_s.at[n], vec_r.at[n], device)

    for n in range(len(others)):
        vec_copy(n).start()

    for n in range(6, steps - 1):
        advance(n)
    mine_in = pl.ds(pl.multiple_of(core * rows_in, 8), rows_in)
    their_in = pl.ds(pl.multiple_of((1 - core) * rows_in, 8), rows_in)
    for j, slot in enumerate(slots):
        @pl.when(chip != slot)
        def _(j=j, slot=slot):
            to = here.device(z=slot // 2, x=slot % 2)
            remote(mix_in.at[j], mix_in.at[j], mix_s.at[0], mix_r.at[j], to).wait_recv()

        @pl.when(chip == slot)
        def _(j=j, slot=slot):
            mix_copies(slot)[0].wait()

        mixf[j] = mix_in[j].astype(FULL)
    mix_pass = remote(mixf.at[:, their_in], mix_swap, ex_s.at[5], ex_r.at[5], partner)
    mix_pass.start()

    for n in range(steps - 1, steps):
        advance(n)

    def last_swap(d):
        return remote(fin.at[d, pl.ds(4, slabs - 4), their_in], swap.at[d], ex_s.at[3 + d], ex_r.at[3 + d], partner)

    for d in range(2):
        last_swap(d).start()
    for d in range(2):
        last_swap(d).wait_recv()
    mix_pass.wait_recv()
    for n in range(len(others)):
        vec_come(n).wait_recv()
    vec_in[me] = pack[me]
    vec_ref[...] = jnp.sum(vec_in[...], axis=0)

    give_cot.wait_send()
    give_ow.wait_send()
    finish_sends()
    for j, slot in enumerate(slots):
        pl.when(chip != slot)(go_copies(j)[1].wait_send)

    @pl.when(has == 1)
    def _():
        for t in range(chips):
            @pl.when(chip != t)
            def _(t=t):
                kv_copies(t)[1].wait_send()
                q_copies(t)[1].wait_send()
                mix_copies(t)[1].wait_send()

    for d in range(2):
        first_swap(d).wait_send()
        last_swap(d).wait_send()
    mix_pass.wait_send()
    for n in range(len(others)):
        vec_copy(n).wait_send()


def finish_kernel(
    nz, act, ing, fin, swap, mixf, mix_swap, vec,
    act_ref, ing_ref, gain1_ref, shift1_ref, mix_ref, mixb_ref, out_ref, outb_ref, gain2_ref, shift2_ref, up_ref, upb_ref,
    dn_ref, dnb_ref,
):
    ny = 2
    core = lax.rem(lax.axis_index("seq"), 2)
    width = ing.shape[2]
    slabs, unit = fin.shape[1], fin.shape[2]
    rows_in = unit // 2
    per_core, head = mixf.shape[0], width // HEADS
    from_row = lax.broadcasted_iota(jnp.int32, (width, width), 0)
    turn = (from_row == natural_of((1, width), 1, rows_in, ny)).astype(LOW)
    mine_in = pl.ds(pl.multiple_of(core * rows_in, 8), rows_in)
    is_first = core == 0

    def by_core(a, b):
        return jnp.where(is_first, a, b), jnp.where(is_first, b, a)

    hidden = (slabs - 5) * fin.shape[3]
    block = hidden // (2 * nz)
    sides = [by_core(mixf[j, mine_in, :], mix_swap[j]) for j in range(per_core)]
    for d in range(2):
        act_ref[d] = dot(act[d], turn, (1, 1)).astype(LOW)
        top_half = jnp.concatenate([fin[d, 0], fin[d, 1]], axis=1)
        low_half = jnp.concatenate([fin[d, 2], fin[d, 3]], axis=1)
        ours = jnp.concatenate([fin[d, s, mine_in, :] for s in range(4, slabs - 1)], axis=1)
        came = jnp.concatenate([swap[d, s] for s in range(slabs - 5)], axis=1)
        one, two = by_core(ours, came)
        blocks = []
        for i in range(hidden // block):
            blocks += [one[:, i * block : (i + 1) * block], two[:, i * block : (i + 1) * block]]
        up_ref[d] = jnp.concatenate(blocks, axis=1)
        one, two = by_core(fin[d, slabs - 1, mine_in, :], swap[d, slabs - 5])
        stacked = [ing[d], top_half, low_half, jnp.concatenate([one, two], axis=1)]
        moved = split_dot(jnp.concatenate(stacked, axis=0), turn, (1, 1))
        span = ing.shape[1]
        ing_ref[d] = moved[:span]
        dn_ref[d] = moved[span : span + 2 * unit]
        out_ref[d] = moved[span + 2 * unit :]
        blocks = []
        for t in range(3):
            for c in range(2):
                for j in range(per_core):
                    start = t * 2 * head + d * head
                    blocks.append(sides[j][c][:, start : start + head])
        mix_ref[d] = jnp.concatenate(blocks, axis=1)
    flat = jnp.concatenate([vec[c : c + 1, :] for c in range(vec.shape[0])], axis=1)
    stride = flat.shape[1] // 2
    smalls = (gain1_ref, shift1_ref, gain2_ref, shift2_ref, outb_ref, dnb_ref, mixb_ref, upb_ref)
    start = 0
    for ref in smalls:
        size = ref.shape[1]
        for d in range(2):
            ref[d : d + 1, :] = flat[:, d * stride + start : d * stride + start + size]
        start += size


def finish(nz, act, ing, fin, swap, mixf, mix_swap, vec):
    width = ing.shape[2]
    slabs, unit, half = fin.shape[1:]
    rows_in = unit // 2
    hidden = (slabs - 5) * half

    def full(*shape):
        return jax.ShapeDtypeStruct((2,) + shape, FULL)

    small = full(rows_in)
    return pl.pallas_call(
        partial(finish_kernel, nz),
        out_shape=(
            jax.ShapeDtypeStruct(act.shape, LOW), jax.ShapeDtypeStruct(ing.shape, FULL), small, small,
            full(rows_in, 3 * width), full(2 * rows_in), full(rows_in, width), small, small, small,
            full(rows_in, 2 * hidden), full(2 * unit), full(2 * unit, width), small,
        ),
        compiler_params=pltpu.CompilerParams(vmem_limit_bytes=60 << 20),
        name="finish",
    )(act, ing, fin, swap, mixf, mix_swap, vec)


def rest(nz, x2, attended, cot, mw_all, up, dn, q, k, v, out_t, top, first_low):
    length, head = q.shape
    _, span, width = cot.shape
    hidden = dn.shape[0]
    half = width // 2
    chips = 2 * nz
    parts = 8 * nz
    rows = 2 * span
    per_core = HEADS // 2
    unit = up.shape[4]
    units = mw_all.shape[:3]
    rows_in = unit // 2
    slabs = 9
    anywhere = pl.BlockSpec(memory_space=pl.ANY)
    vmem = pl.BlockSpec(memory_space=pltpu.VMEM)
    low, full = partial(pltpu.VMEM, dtype=LOW), partial(pltpu.VMEM, dtype=FULL)
    return pl.pallas_call(
        partial(rest_kernel, nz, 512),
        out_shape=(
            jax.ShapeDtypeStruct((2, span, width), LOW),
            jax.ShapeDtypeStruct((2, span, width), FULL),
            jax.ShapeDtypeStruct((2, slabs, unit, half), FULL),
            jax.ShapeDtypeStruct((2, slabs - 4, rows_in, half), FULL),
            jax.ShapeDtypeStruct((per_core, unit, half), FULL),
            jax.ShapeDtypeStruct((per_core, rows_in, half), FULL),
            jax.ShapeDtypeStruct((5, 128), FULL),
        ),
        in_specs=[vmem] * 3 + [anywhere] * 3 + [vmem] * 5 + [anywhere],
        out_specs=[vmem] * 7,
        scratch_shapes=[
            low(units + (unit, hidden)),
            low((hidden, width)),
            low((2,) + units + (unit, half)),
            low((width, width)),
            low((width, width)),
            low(units + (16, half)),
            low((rows, width)),
            low((2, rows, width)),
            low((2, rows, width)),
            low((2, rows, hidden)),
            low((2, rows, hidden)),
            full((rows, width)),
            full((2, rows, width)),
            full((2, span, width)),
            full((2, rows, width)),
            full((2, span, width)),
            full((2, span, width)),
            low((2, rows, width)),
            low((2,) + units + (slabs, unit, half)),
            low((per_core, rows, 2 * head)),
            low((chips, rows, 2 * head)),
            low((head, length)),
            low((2, head, length)),
            full((2, 1, length)),
            full((2, head, length)),
            low((chips, 3, rows, 2 * head)),
            low((per_core, 3, rows, 2 * head)),
            low(units + (per_core // 2 * unit, half)),
            low((2, rows, width)),
            full((width, half)),
            low(units + (unit, half)),
            low((nz, 2, unit, half)),
            low((per_core, unit, half)),
            low((2, nz, 2, slabs, unit, half)),
            low((2, nz, slabs, unit, half)),
            low((2, nz + 1, slabs, unit, half)),
            full((parts, 5, 128)),
            full((parts, 5, 128)),
            DMA((8,)),
            DMA((8,)),
            DMA((8,)),
            DMA((2,)),
            DMA((per_core,)),
            DMA((chips,)),
            DMA((chips,)),
            DMA((per_core,)),
            DMA((chips,)),
            DMA((per_core,)),
            DMA((2, nz, 3)),
            DMA((2, nz, 3)),
            DMA((2, nz, 3)),
            DMA((2, nz, 3)),
            DMA((2, nz, 3)),
            DMA((2, 2, nz, 3)),
            DMA((6,)),
            DMA((6,)),
            DMA((parts - 1,)),
            DMA((parts - 1,)),
            DMA((chips,)),
            DMA((per_core,)),
        ],
        compiler_params=pltpu.CompilerParams(vmem_limit_bytes=62 << 20, collective_id=1, has_side_effects=True),
        cost_estimate=pl.CostEstimate(
            flops=60 * rows * width * hidden, bytes_accessed=60 * width * hidden, transcendentals=length * length
        ),
        name="rest",
    )(x2, attended, cot, mw_all, up, dn, q, k, v, out_t, top, first_low)


def plain_on_device(
    inputs,
    attend_gain,
    attend_shift,
    mixing_weight,
    mixing_bias,
    output_weight,
    output_bias,
    feed_gain,
    feed_shift,
    up_weight,
    up_bias,
    down_weight,
    down_bias,
    cotangent,
):
    place = Place()
    _, span, width = inputs.shape
    nz, ny, core, chip = place.nz, place.ny, place.core, place.chip
    chips = nz * 2
    parts = chips * 2 * ny
    head = width // HEADS
    per_core = HEADS // 2
    slots = [int((j + 0.5) * chips / per_core) for j in range(per_core)]
    half = width // 2
    hidden = up_weight.shape[1]
    rows_in = width // parts
    rows_hid = hidden // parts
    groups = [[2 * i + c for i in range(chips)] for c in range(2)]

    def exchange(values):
        return lax.all_to_all(values, "seq", 0, 0, axis_index_groups=groups, tiled=True)

    def spread(blocks):
        filled = [jnp.zeros_like(blocks[0])] * chips
        for j, slot in enumerate(slots):
            filled[slot] = blocks[j]
        return jnp.stack(filled)

    def collect(blocks):
        return jnp.stack([blocks[slot] for slot in slots])

    owned = [-1] * chips
    for j, slot in enumerate(slots):
        owned[slot] = j
    my_head = jnp.array(owned, jnp.int32)[chip]
    busy = (my_head >= 0).astype(FULL)
    my_head = jnp.maximum(my_head, 0)

    def by_core(values, dim):
        mine = lax.dynamic_index_in_dim(values, core, dim, keepdims=False)
        theirs = lax.dynamic_index_in_dim(values, 1 - core, dim, keepdims=False)
        return mine, theirs

    vectors = jnp.concatenate(
        [attend_gain, attend_shift, feed_gain, feed_shift, output_bias, down_bias, mixing_bias, up_bias]
    )
    vectors = place.both(vectors, vectors)
    vectors = place.gather(vectors, "z", 0)
    vectors = place.gather(vectors, "x", 1)
    vectors = place.gather(vectors, "y", 3)
    vectors = vectors.reshape(parts, -1).astype(FULL)
    cuts = [vectors[:, i * rows_in : (i + 1) * rows_in].reshape(-1) for i in range(6)]
    first_gain, first_shift, second_gain, second_shift, out_bias, down_bias_all = cuts
    mix_bias = vectors[:, 6 * rows_in : 8 * rows_in].reshape(2, HEADS, head)
    up_bias_all = vectors[:, 8 * rows_in :].reshape(chips, 2, ny * rows_hid)
    up_bias_mine = lax.dynamic_index_in_dim(up_bias_all, core, 1, keepdims=False).reshape(-1)

    own = inputs.reshape(span, width)
    column = [own] + [place.send(own, "z", d) for d in range(1, nz)]
    beside = [place.send(piece, "x") for piece in column]
    x_all = jnp.zeros((nz, 2, span, width), LOW)
    for d in range(nz):
        at = lax.rem(place.z + nz - d, nz)
        x_all = lax.dynamic_update_slice(x_all, column[d][None, None], (at, place.x, 0, 0))
        x_all = lax.dynamic_update_slice(x_all, beside[d][None, None], (at, 1 - place.x, 0, 0))
    x_all = place.both(x_all, x_all).transpose(1, 2, 0, 3, 4)
    x_all = x_all.reshape(chips * 2 * span, width)

    def gather_rows(mine, theirs):
        block = place.both(mine, theirs)
        block = place.gather(block, "z", 0)
        block = place.gather(block, "x", 1)
        block = place.gather(block, "y", 3)
        return block.reshape(parts * block.shape[-2], block.shape[-1])

    mixing = mixing_weight.reshape(rows_in, 3, 2, half)
    mine, theirs = by_core(mixing, 2)
    mixing = gather_rows(mine.reshape(rows_in, -1), theirs.reshape(rows_in, -1))
    mine, theirs = by_core(output_weight.reshape(rows_in, 2, half), 1)
    out_half = gather_rows(mine, theirs)
    out_all = place.both(out_half, out_half).transpose(1, 0, 2).reshape(width, width)
    mine, theirs = by_core(up_weight.reshape(rows_in, chips, 2, ny * rows_hid), 2)
    up = gather_rows(mine.reshape(rows_in, -1), theirs.reshape(rows_in, -1))
    down = place.gather(down_weight, "z", 0)
    down = place.gather(down, "x", 1)
    down = place.gather(down, "y", 2).reshape(chips * ny * rows_hid, width)

    mixing = mixing.reshape(width, 3, per_core, head)
    head_weight = lax.dynamic_index_in_dim(mixing, my_head, 2, keepdims=False).reshape(width, 3 * head)
    whole_head = core * per_core + my_head
    head_bias = lax.dynamic_index_in_dim(mix_bias, whole_head, 1, keepdims=False)
    head_bias = jnp.concatenate([head_bias[0], jnp.zeros((head,), FULL), head_bias[1]])
    first_low, q, k, v, out, out_t, top = attend_plain(
        x_all, first_gain[None], first_shift[None], head_weight, head_bias[None]
    )
    attended = collect(exchange(out.reshape(chips, 2 * span, head)))
    attended = attended.transpose(1, 0, 2).reshape(2 * span, half)
    attended = place.both(attended, attended).transpose(1, 0, 2).reshape(2 * span, width)

    residual = lax.dynamic_slice_in_dim(x_all, chip * 2 * span, 2 * span, 0).astype(FULL)
    branch = dot(attended, out_all, (1, 0)) + out_bias
    scale = jnp.array(SCALES, FULL)[:, None, None]
    middle = residual + scale * branch
    second_normed, second_inv = normalize(middle)
    second_low = (second_normed * second_gain + second_shift).astype(LOW)
    rows = second_low.reshape(4 * span, width)
    hidden_pre = dot(rows, up, (1, 0)) + up_bias_mine
    activated, gelu_back = jax.vjp(partial(jax.nn.gelu, approximate=True), hidden_pre)
    activated_low = activated.astype(LOW)
    feed_part = dot(activated_low, down, (1, 0)).reshape(2, 2, span, width)
    mine, theirs = by_core(feed_part, 1)
    feed_own = mine + place.send(theirs, "core") + down_bias_all

    def own_rows(values):
        return lax.dynamic_index_in_dim(
            values.reshape((2, 2, span) + values.shape[2:]), core, 1, keepdims=False
        )

    activations = (own_rows(middle) + scale * feed_own).astype(LOW)
    upstream_own = cotangent.reshape(2, span, width)
    upstream = place.both(upstream_own, upstream_own).transpose(1, 0, 2, 3)
    down_in = (scale[..., None] * upstream.astype(FULL)).astype(LOW).reshape(4 * span, width)
    hidden_low = gelu_back(dot(down_in, down, (1, 1)))[0].astype(LOW)
    second_part = dot(hidden_low, up, (1, 1)).reshape(2, 2, span, width)
    mine, theirs = by_core(second_part, 1)
    second_grad = mine + place.send(theirs, "core")
    normed_own, inv_own = own_rows(second_normed), own_rows(second_inv)
    middle_grad = upstream_own.astype(FULL) + norm_back(second_grad, normed_own, inv_own, second_gain)
    branch_own = (scale * middle_grad).astype(LOW)
    branch_low = place.both(branch_own, branch_own).transpose(1, 0, 2, 3).reshape(2, 2 * span, width)
    out_rows = lax.dynamic_slice_in_dim(out_all, core * half, half, 0)
    go = dot(branch_low.reshape(4 * span, width), out_rows, (1, 1)).astype(LOW)
    go = go.reshape(2, 2 * span, per_core, head).transpose(2, 1, 0, 3).reshape(per_core, 2 * span, 2 * head)
    go = exchange(spread(go)).reshape(chips * 2 * span, 2 * head)

    gq, gk, gv = attend_back(q, k, v, out_t, top, go)
    head_grads = jnp.concatenate([gq, gk, gv], axis=1)

    depth_rows = second_low.reshape(2, 2 * span, width)
    hidden_rows = hidden_low.reshape(2, 2 * span, -1)
    active_rows = activated_low.reshape(2, 2 * span, -1)
    in_rows = down_in.reshape(2, 2 * span, width)
    branch_cols = lax.dynamic_slice_in_dim(branch_low, core * half, half, 2)
    orders = (("y", "x"), ("x", "y"))

    def scatter_chips(values, order):
        dims = {"x": 1, "y": 2}
        values = place.scatter(values, order[0], dims[order[0]]).astype(LOW)
        values = place.scatter(values, order[1], 1).astype(LOW)
        return place.scatter(values, "z", 0)

    def scatter_rows(values, order):
        shaped = values.reshape(nz, 2, 2, ny, rows_in, -1).transpose(0, 1, 3, 2, 4, 5)
        summed = scatter_chips(shaped, order)
        mine, theirs = by_core(summed, 0)
        return place.both(mine, theirs)

    down_grads, up_grads, out_grads = [], [], []
    for depth in range(2):
        grad = dot(active_rows[depth], in_rows[depth], (0, 0)).astype(LOW)
        down_grads.append(scatter_chips(grad.reshape(nz, 2, ny, rows_hid, width), orders[depth]))
    for depth in range(2):
        grad = dot(depth_rows[depth], hidden_rows[depth], (0, 0)).astype(LOW)
        grad = scatter_rows(grad, orders[depth]).reshape(2, rows_in, chips, -1)
        up_grads.append(grad.transpose(1, 2, 0, 3).reshape(rows_in, hidden))
    for depth in range(2):
        grad = dot(attended, branch_cols[depth], (0, 0)).astype(LOW)
        out_grads.append(scatter_rows(grad, orders[depth]).transpose(1, 0, 2).reshape(rows_in, width))

    head_sum = dot(first_low, head_grads, (0, 0)).astype(LOW).reshape(nz, 2, 2, ny, rows_in, 6 * head)
    head_sum = place.scatter(head_sum, "y", 3).astype(LOW).reshape(chips, 2, rows_in, 6 * head)
    head_sum = collect(exchange(head_sum))
    mine, theirs = by_core(head_sum, 1)
    mixing_grad = place.both(mine, theirs).reshape(HEADS, rows_in, 3, 2, head)
    mixing_grad = mixing_grad.transpose(3, 1, 2, 0, 4).reshape(2, rows_in, 3 * width).astype(FULL)

    mixed_grads = collect(exchange(head_grads.reshape(chips, 2 * span, 6 * head)))
    mixed_grads = mixed_grads.reshape(per_core, 2 * span, 3, 2, head).transpose(3, 1, 2, 0, 4)
    mixed_grads = mixed_grads.reshape(4 * span, 3 * half)
    first_part = dot(mixed_grads, mixing.reshape(width, 3 * half), (1, 1)).reshape(2, 2, span, width)
    mine, theirs = by_core(first_part, 1)
    first_grad = mine + place.send(theirs, "core")
    first_normed, first_inv = normalize(own.astype(FULL))
    input_grad = middle_grad + norm_back(first_grad, first_normed, first_inv, first_gain)

    bias_sum = jnp.sum(head_grads.astype(FULL), axis=0).reshape(3, 2, head) * busy
    spot = (jnp.arange(HEADS) == whole_head).astype(FULL)[None, None, :, None]
    bias_sum = (jnp.stack([bias_sum[0], bias_sum[2]], axis=1)[:, :, None, :] * spot).reshape(2, parts, -1)
    hidden_sum = jnp.sum(hidden_rows.astype(FULL), axis=1).reshape(2, chips, 1, ny * rows_hid)
    hidden_spot = (jnp.arange(2) == core).astype(FULL)[None, None, :, None]
    hidden_sum = (hidden_sum * hidden_spot).reshape(2, parts, rows_hid)
    in_own = (scale * upstream_own.astype(FULL)).astype(LOW)
    sums = [
        jnp.sum(first_grad * first_normed, axis=1),
        jnp.sum(first_grad, axis=1),
        jnp.sum(second_grad * normed_own, axis=1),
        jnp.sum(second_grad, axis=1),
        jnp.sum(branch_own.astype(FULL), axis=1),
        jnp.sum(in_own.astype(FULL), axis=1),
    ]
    sums = [item.reshape(2, parts, rows_in) for item in sums] + [bias_sum, hidden_sum]
    sums = jnp.concatenate(sums, axis=2).reshape(2, nz, 2, 2, ny, -1)
    sums = place.scatter(sums, "y", 4)
    sums = place.scatter(sums, "x", 2)
    sums = place.scatter(sums, "core", 2)
    sums = place.scatter(sums, "z", 1)
    small = [sums[:, i * rows_in : (i + 1) * rows_in] for i in range(6)]
    return (
        activations[:, None],
        input_grad[:, None],
        small[0],
        small[1],
        mixing_grad,
        sums[:, 6 * rows_in : 8 * rows_in],
        jnp.stack(out_grads),
        small[4],
        small[2],
        small[3],
        jnp.stack(up_grads),
        sums[:, 8 * rows_in :],
        jnp.stack(down_grads),
        small[5],
    )


def on_device(
    inputs,
    attend_gain,
    attend_shift,
    mixing_weight,
    mixing_bias,
    output_weight,
    output_bias,
    feed_gain,
    feed_shift,
    up_weight,
    up_bias,
    down_weight,
    down_bias,
    cotangent,
):
    place = Place()
    _, span, width = inputs.shape
    nz, ny, core, chip = place.nz, place.ny, place.core, place.chip
    chips = nz * 2
    parts = chips * 2 * ny
    head = width // HEADS
    per_core = HEADS // 2
    half = width // 2
    hidden = up_weight.shape[1]
    rows_in = width // parts
    rows_hid = hidden // parts
    groups = [[2 * i + c for i in range(chips)] for c in range(2)]

    def by_core(values, dim):
        mine = lax.dynamic_index_in_dim(values, core, dim, keepdims=False)
        theirs = lax.dynamic_index_in_dim(values, 1 - core, dim, keepdims=False)
        return mine, theirs

    own = inputs.reshape(span, width)
    pairs = per_core // 2
    mix = mixing_weight.reshape(rows_in, 3, 2, pairs, 2, head).transpose(2, 3, 0, 1, 4, 5)
    mix = mix.reshape(2, pairs, rows_in, half)
    out_cols = output_weight.reshape(rows_in, 2, half).transpose(1, 0, 2)[:, None]
    vectors, start = jnp.zeros((half,), LOW), 0
    for piece in (
        attend_gain, attend_shift, feed_gain, feed_shift, output_bias, down_bias, mixing_bias, up_bias
    ):
        vectors = vectors + jnp.pad(piece, (start, half - start - piece.shape[0]))
        start += piece.shape[0]
    vectors = jnp.broadcast_to(jnp.pad(vectors[None], ((0, 7), (0, 0))), (2, 8, half))
    packed = jnp.concatenate([mix.reshape(2, pairs * rows_in, half), out_cols[:, 0], vectors], axis=1)
    up_cols = up_weight.reshape(rows_in, chips, 2, ny * rows_hid).transpose(2, 0, 1, 3).reshape(2, rows_in, -1)
    mine, theirs = by_core(packed, 0)
    packed = place.both(mine, theirs)
    cut = pairs * rows_in
    pair_rows = packed[:, :cut].reshape(2, pairs, rows_in, half).transpose(1, 0, 2, 3).reshape(2 * cut, half)
    packed_rows = jnp.concatenate([pair_rows, packed[:, cut + rows_in :].reshape(16, half)])
    mine, theirs = by_core(up_cols, 0)
    up_unit = place.both(mine, theirs).reshape(2 * rows_in, -1, half).transpose(1, 0, 2)
    up_unit = jnp.concatenate([up_unit, packed[:, cut : cut + rows_in].reshape(1, 2 * rows_in, half)])

    mw_all, up_all, dn_all, first_low, q, k, v, out_t, top, attended, x2 = attend(
        nz, ny, own, packed_rows, up_unit, down_weight
    )

    raw = rest(
        nz, x2.reshape(2 * span, width), attended, cotangent.reshape(2, span, width), mw_all,
        up_all, dn_all.reshape(-1, width), q, k, v, out_t, top, first_low,
    )
    activations, input_grad, *others = finish(nz, *raw)
    return (activations[:, None], input_grad[:, None], *others)


def tiles_well(mesh):
    ny, seq = mesh.shape["batch"], mesh.shape["seq"]
    rows_in = 768 // (seq * ny)
    return ny == 2 and seq // 2 >= HEADS // 2 and 2 * rows_in % 16 == 0 and 2 * rows_in * seq * ny == 2 * 768


def solution(mesh):
    shard = P(("seq", "batch"))
    grad = P(None, ("seq", "batch"))
    row = P(None, "batch", "seq", None)
    return jax.shard_map(
        on_device if tiles_well(mesh) else plain_on_device,
        mesh=mesh,
        in_specs=(P("batch", "seq", None),) + (shard,) * 12 + (row,),
        out_specs=(row, row) + (grad,) * 12,
        check_vma=False,
    )
```

profile of v0, /device:TPU:11, one launch (start us, length us, event | category | flops | bytes accessed | tf_op | source)
XLA Modules:
  0.0 266.4 jit_solution(4052655370121996721)
XLA Ops:
  0.6 1.1 reshape.73
  1.8 0.2 reshape.74
  2.0 0.7 collective-permute-start.1
  2.8 0.9 pad_add_fusion
  3.6 0.8 copy.53
  4.4 1.1 reshape.68
  5.5 0.2 copy.50
  5.6 0.2 reshape_reshape.3
  5.9 0.1 collective-permute-start
  6.0 0.0 collective-permute-done.1
  6.2 1.1 collective-permute-done
  7.4 0.7 pad_maximum_fusion.3.mw_ref
  8.0 0.7 pad_maximum_fusion.up_ref
  8.7 92.4 %attend.1 = (bf16[4,2,2,160,384]{4,3,2,1,0:T(8,128)(2,1)}, bf16[4,2,2,5,48,384]{5,4,3,2,1,0:T(8,128)(2,1)}, bf16[4,2,2,96,768]{4,3,2,1,0:T(8,128)(2,1)}, bf16[20...) custom-call(bf16[128,768]{1,0:T(8,128)(2,1)} %bitcast.72, ...), custom_call_target="tpu_custom_call" | custom-call | flops 1610612736 | bytes 12582912 | tf_op jit(solution)/shard_map/attend/pallas_call | solution.py:687
  101.2 158.8 %rest.1 = (bf16[2,128,768]{2,1,0:T(8,128)(2,1)}, f32[2,128,768]{2,1,0:T(8,128)}, f32[2,9,48,384]{3,2,1,0:T(8,128)}, f32[2,5,24,384]{3,2,1,0:T(8,128)}, f32[6,48,...) custom-call(bf16[256,768]{1,0:T(8,128)(2,1)} %bitcast.74, ...), custom_call_target="tpu_custom_call" | custom-call | flops 18119393280 | bytes 70778880 | tf_op jit(solution)/shard_map/rest/pallas_call | solution.py:1488
  259.9 6.3 %finish.1 = (bf16[2,128,768]{2,1,0:T(8,128)(2,1)}, f32[2,128,768]{2,1,0:T(8,128)}, f32[2,24]{1,0:T(2,128)}, f32[2,24]{1,0:T(2,128)}, f32[2,24,2304]{2,1,0:T(8,12...) custom-call(bf16[2,128,768]{2,1,0:T(8,128)(2,1)} %get-tuple-element., ...), custom_call_target="tpu_custom_call" | custom-call | tf_op jit(solution)/shard_map/finish/pallas_call | solution.py:1460
  (16 shorter events, 0.3 us)
Async XLA Ops:
  2.0 4.0 %collective-permute-start.1 = (bf16[24,1536]{1,0:T(8,128)(2,1)S(1)}, bf16[24,1536]{1,0:T(8,128)(2,1)S(1)}, u32[]{:S(2)}, u32[]{:S(2)}) collective-permute-start(bf16[24,1536]{1,0:T(8,128)(2,1)S(1)} %dynamic-slice_bitcast_fusion.1), channel_id=1, source_target_pairs={{0,2},{1,3},{2,0},{3,1},{4,6},{5,7},{6,4},{7,5},{8,10},{9,11},{10,... | collective-permute-start | bytes 221192 | tf_op jit(solution)/shard_map/ppermute | solution.py:68
  5.9 1.3 collective-permute-start
where the time goes:
time: 270 us; the launch traced here: 266 us
  Pallas kernels  257 us (95%)
  local copies, waits for them, and re-layouts  3.66 us (1%)
    pallas_call x1, Pallas kernels, rest(): pl.pallas_call(partial(rest_kernel, nz, 512), out_shape=(jax.ShapeDtypeSt...  159 us
    pallas_call x1, Pallas kernels, attend(): pl.pallas_call(partial(attend_kernel, nz, ny), out_shape=(jax.ShapeDtypeS...  92.4 us
    pallas_call x1, Pallas kernels, finish(): pl.pallas_call(partial(finish_kernel, nz), out_shape=(jax.ShapeDtypeStruc...  6.28 us
  transfers between devices with their start and end apart: 2, of which 1 were waited for; matrix products, arithmetic and copies ran while one was open for 1% of the time, Pallas kernels for 0%

commit v1 on v0

--- a/solution.py
+++ b/solution.py
@@ -479,7 +479,7 @@
 def attend_kernel(
     nz, ny, x_ref, mw_ref, up_ref, dn_ref,
     mw_all, up_all, dn_all, h_ref, q_ref, k_ref, v_ref, ot_ref, top_ref, att_ref, x2_ref,
-    xs, wt, vc, vt_ref, o_ref, pm, x_own, up_own, dn_own, load, att_s, att_r, pass_s, pass_r, *sems,
+    xs, wt, vc, vt_ref, o_ref, pm, x_own, up_own, dn_own, xn, flat_ref, load, att_s, att_r, pass_s, pass_r, *sems,
 ):
     here = Here(nz, ny)
     chips = 2 * nz
@@ -543,6 +543,17 @@
     then(first, nz - 1, "second")
     take(later, 0)
     for k in range(nz):
+        then((rows,), k, "third")
+    rows.kept.wait()
+    keep_rows = pltpu.make_async_copy(xs.at[here.z, here.x], x2_ref, load.at[2])
+    keep_rows.start()
+
+    @pl.when(has == 1)
+    def _():
+        for i in range(chips):
+            xn[i], _ = normalize(xs[i // 2, i % 2].reshape(tile, width).astype(FULL))
+
+    for k in range(nz):
         then((mw,), k, "third")
     mw.kept.wait()
     my_pair = pl.ds(pl.multiple_of(lax.div(mine, 2) * unit, unit), unit)
@@ -550,13 +561,8 @@
     pair.start()
     vectors = pltpu.make_async_copy(mw_all.at[:, :, :, pl.ds(pair_rows, 16)], vc, load.at[1])
     vectors.start()
-    for k in range(nz):
-        then((rows,), k, "third")
-    rows.kept.wait()
     pair.wait()
     vectors.wait()
-    keep_rows = pltpu.make_async_copy(xs.at[here.z, here.x], x2_ref, load.at[2])
-    keep_rows.start()
 
     steps = []
     for k in range(1, nz):
@@ -582,25 +588,21 @@
         spot = lax.broadcasted_iota(jnp.int32, (pieces.shape[1], cols.shape[1]), 0)
         moved = dot(pieces, (spot == cols).astype(LOW), (1, 0))
         from_row = lax.broadcasted_iota(jnp.int32, moved.shape, 0)
-        flat = jnp.sum(jnp.where(from_row == owners, moved, 0.0), axis=0, keepdims=True)
-        gain, shift, bias = flat[:, :width], flat[:, width : 2 * width], flat[:, 2 * width :]
-        weight = wt[...].reshape(width, -1)
-
-        def choose(values):
-            return jnp.where(odd, values[:, head:], values[:, :head])
-
-        for i in range(chips):
-            span = slice(i * tile, (i + 1) * tile)
-            values = xs[i // 2, i % 2].reshape(tile, width).astype(FULL)
-            normed, _ = normalize(values)
-            low = (normed * gain + shift).astype(LOW)
-            h_ref[span, :] = low
-            mixed = (dot(low, weight, (1, 0)) + bias).astype(LOW)
-            q_ref[span, :] = (choose(mixed[:, : 2 * head]) * (head ** (-0.5))).astype(LOW)
-            k_ref[span, :] = choose(mixed[:, 2 * head : 4 * head])
-            value = choose(mixed[:, 4 * head :])
-            v_ref[span, :] = value
-            vt_ref[:, span] = value.T
+        flat_ref[...] = jnp.sum(jnp.where(from_row == owners, moved, 0.0), axis=0, keepdims=True)
+
+    def choose(values):
+        return jnp.where(odd, values[:, head:], values[:, :head])
+
+    def project(i):
+        span = slice(i * tile, (i + 1) * tile)
+        low = (xn[i] * flat_ref[:, :width] + flat_ref[:, width : 2 * width]).astype(LOW)
+        h_ref[span, :] = low
+        mixed = (dot(low, wt[...].reshape(width, -1), (1, 0)) + flat_ref[:, 2 * width :]).astype(LOW)
+        q_ref[span, :] = (choose(mixed[:, : 2 * head]) * (head ** (-0.5))).astype(LOW)
+        k_ref[span, :] = choose(mixed[:, 2 * head : 4 * head])
+        value = choose(mixed[:, 4 * head :])
+        v_ref[span, :] = value
+        vt_ref[:, span] = value.T
 
     def query_tile(i):
         span = slice(i * tile, (i + 1) * tile)
@@ -636,6 +638,11 @@
             pltpu.make_async_copy(o_ref.at[i], spot, att_s.at[i]),
             remote(o_ref.at[i], spot, att_s.at[i], att_r.at[mine], here.device(z=i // 2, x=i % 2)),
         )
+
+    @pl.when(has == 1)
+    def _():
+        for i in range(chips):
+            project(i)
 
     for i in range(chips):
         @pl.when(has == 1)
@@ -711,6 +718,8 @@
             pltpu.VMEM(own.shape, LOW),
             pltpu.VMEM(up.shape, LOW),
             pltpu.VMEM(dn.shape, LOW),
+            pltpu.VMEM((2 * nz, 2 * span, width), FULL),
+            pltpu.VMEM((1, 2 * width + width // 2), FULL),
             DMA((3,)),
             DMA((2 * nz,)),
             DMA((HEADS // 2,)),

time: 270 us -> 270 us (level)
  no operation moved by 1% of the time
where the time goes in v1:
time: 270 us; the launch traced here: 266 us
  Pallas kernels  257 us (95%)
  local copies, waits for them, and re-layouts  3.66 us (1%)
    pallas_call x1, Pallas kernels, rest(): pl.pallas_call(partial(rest_kernel, nz, 512), out_shape=(jax.ShapeDtypeSt...  160 us
    pallas_call x1, Pallas kernels, attend(): pl.pallas_call(partial(attend_kernel, nz, ny), out_shape=(jax.ShapeDtypeS...  90.8 us
    pallas_call x1, Pallas kernels, finish(): pl.pallas_call(partial(finish_kernel, nz), out_shape=(jax.ShapeDtypeStruc...  6.27 us
  transfers between devices with their start and end apart: 2, of which 1 were waited for; matrix products, arithmetic and copies ran while one was open for 1% of the time, Pallas kernels for 0%

profile of v1, /device:TPU:11, one launch (start us, length us, event | category | flops | bytes accessed | tf_op | source)
XLA Modules:
  0.0 265.9 jit_solution(199142919739389572)
XLA Ops:
  0.6 1.1 reshape.73
  1.8 0.2 reshape.74
  2.0 0.7 collective-permute-start.1
  2.8 0.9 pad_add_fusion
  3.6 0.8 copy.53
  4.4 1.1 reshape.68
  5.5 0.2 copy.50
  5.6 0.2 reshape_reshape.3
  5.9 0.1 collective-permute-start
  6.0 0.0 collective-permute-done.1
  6.2 1.1 collective-permute-done
  7.4 0.7 pad_maximum_fusion.3.mw_ref
  8.0 0.7 pad_maximum_fusion.up_ref
  8.7 90.8 %attend.1 = (bf16[4,2,2,160,384]{4,3,2,1,0:T(8,128)(2,1)}, bf16[4,2,2,5,48,384]{5,4,3,2,1,0:T(8,128)(2,1)}, bf16[4,2,2,96,768]{4,3,2,1,0:T(8,128)(2,1)}, bf16[20...) custom-call(bf16[128,768]{1,0:T(8,128)(2,1)} %bitcast.72, ...), custom_call_target="tpu_custom_call" | custom-call | flops 1610612736 | bytes 12582912 | tf_op jit(solution)/shard_map/attend/pallas_call | solution.py:694
  99.6 159.8 %rest.1 = (bf16[2,128,768]{2,1,0:T(8,128)(2,1)}, f32[2,128,768]{2,1,0:T(8,128)}, f32[2,9,48,384]{3,2,1,0:T(8,128)}, f32[2,5,24,384]{3,2,1,0:T(8,128)}, f32[6,48,...) custom-call(bf16[256,768]{1,0:T(8,128)(2,1)} %bitcast.74, ...), custom_call_target="tpu_custom_call" | custom-call | flops 18119393280 | bytes 70778880 | tf_op jit(solution)/shard_map/rest/pallas_call | solution.py:1497
  259.4 6.3 %finish.1 = (bf16[2,128,768]{2,1,0:T(8,128)(2,1)}, f32[2,128,768]{2,1,0:T(8,128)}, f32[2,24]{1,0:T(2,128)}, f32[2,24]{1,0:T(2,128)}, f32[2,24,2304]{2,1,0:T(8,12...) custom-call(bf16[2,128,768]{2,1,0:T(8,128)(2,1)} %get-tuple-element., ...), custom_call_target="tpu_custom_call" | custom-call | tf_op jit(solution)/shard_map/finish/pallas_call | solution.py:1469
  (16 shorter events, 0.3 us)
Async XLA Ops:
  2.0 4.0 %collective-permute-start.1 = (bf16[24,1536]{1,0:T(8,128)(2,1)S(1)}, bf16[24,1536]{1,0:T(8,128)(2,1)S(1)}, u32[]{:S(2)}, u32[]{:S(2)}) collective-permute-start(bf16[24,1536]{1,0:T(8,128)(2,1)S(1)} %dynamic-slice_bitcast_fusion.1), channel_id=1, source_target_pairs={{0,2},{1,3},{2,0},{3,1},{4,6},{5,7},{6,4},{7,5},{8,10},{9,11},{10,... | collective-permute-start | bytes 221192 | tf_op jit(solution)/shard_map/ppermute | solution.py:68
  5.9 1.3 collective-permute-start

commit v2 on v1

--- a/solution.py
+++ b/solution.py
@@ -478,7 +478,8 @@
 
 def attend_kernel(
     nz, ny, x_ref, mw_ref, up_ref, dn_ref,
-    mw_all, up_all, dn_all, h_ref, q_ref, k_ref, v_ref, ot_ref, top_ref, att_ref, x2_ref,
+    mw_all, up_all, dn_all, h_all, q_all, k_all, v_all, ot_all, top_all, att_ref, x2_ref,
+    h_ref, q_ref, k_ref, v_ref, ot_ref, top_ref, out_s,
     xs, wt, vc, vt_ref, o_ref, pm, x_own, up_own, dn_own, xn, flat_ref, load, att_s, att_r, pass_s, pass_r, *sems,
 ):
     here = Here(nz, ny)
@@ -639,10 +640,15 @@
             remote(o_ref.at[i], spot, att_s.at[i], att_r.at[mine], here.device(z=i // 2, x=i % 2)),
         )
 
+    pairs_out = (h_ref, h_all), (q_ref, q_all), (k_ref, k_all), (v_ref, v_all), (ot_ref, ot_all), (top_ref, top_all)
+    leaving = [pltpu.make_async_copy(src, dst, out_s.at[i]) for i, (src, dst) in enumerate(pairs_out)]
+
     @pl.when(has == 1)
     def _():
         for i in range(chips):
             project(i)
+        for copy in leaving[:4]:
+            copy.start()
 
     for i in range(chips):
         @pl.when(has == 1)
@@ -663,6 +669,13 @@
             stay, leave = hand(i)
             pl.when(here.chip == i)(stay.wait)
             pl.when(here.chip != i)(leave.wait_send)
+
+    @pl.when(has == 1)
+    def _():
+        for copy in leaving[4:]:
+            copy.start()
+        for copy in leaving:
+            copy.wait()
 
     for j, slot in enumerate(slots):
         @pl.when(here.chip != slot)
@@ -707,8 +720,15 @@
             jax.ShapeDtypeStruct((2, span, width), LOW),
         ),
         in_specs=[vmem] * 4,
-        out_specs=[anywhere] * 3 + [vmem] * 6 + [anywhere] * 2,
+        out_specs=[anywhere] * 11,
         scratch_shapes=[
+            pltpu.VMEM((length, width), LOW),
+            pltpu.VMEM((length, head), LOW),
+            pltpu.VMEM((length, head), LOW),
+            pltpu.VMEM((length, head), LOW),
+            pltpu.VMEM((head, length), FULL),
+            pltpu.VMEM((1, length), FULL),
+            DMA((6,)),
             pltpu.VMEM((nz, 2, 2, span, width), LOW),
             pltpu.VMEM(units + up.shape[1:], LOW),
             pltpu.VMEM(units + (16,) + mw.shape[1:], LOW),
@@ -759,11 +779,11 @@
 def rest_kernel(
     nz, hidden_tile,
     x2_ref, att_ref, cot_ref, mw_all, up_ref, dn_ref,
-    q_ref, k_ref, v_ref, ot_ref, top_ref, h_all,
+    q_all, k_all, v_all, ot_all, top_all, h_all,
     act_ref, ing_ref, fin, swap, mixf, mix_swap, vec_ref,
     up, dn, ow, own, pm, vc, att, cot, h2, act_low, gu, branch, feed, feed_in, gh2, gh2_in, gmid, eb, grads, go_send,
     go_all, kt_ref, got_ref, delta_ref, gqt_ref, gsend, gat, mw, hbuf, head_acc, head_sum, hs_in, mix_in,
-    r1, r2, r3, pack, vec_in,
+    r1, r2, r3, pack, vec_in, q_ref, k_ref, v_ref, ot_ref, top_ref, in_s,
     load, near_s, near_r, h_s, go_s, go_r, kv_s, kv_r, q_s, q_r, s1, t1, s2, t2, s3, t3, ex_s, ex_r,
     vec_s, vec_r, mix_s, mix_r,
 ):
@@ -817,6 +837,10 @@
     for copy in loads:
         copy.start()
     met = greet([device for device, _, _ in others])
+    pairs_in = (q_all, q_ref), (k_all, k_ref), (v_all, v_ref), (ot_all, ot_ref), (top_all, top_ref)
+    entering = [pltpu.make_async_copy(src, dst, in_s.at[i]) for i, (src, dst) in enumerate(pairs_in)]
+    for copy in entering:
+        copy.start()
 
     def pass_on(i, src, dst):
         return remote(src, dst, near_s.at[i], near_r.at[i], partner)
@@ -1140,6 +1164,9 @@
     for c in range(pack.shape[1]):
         pack[:, c, :] = total[:, c * 128 : (c + 1) * 128]
     advance(0)
+
+    for copy in entering:
+        copy.wait()
 
     def h_copy(i):
         rows = slice(i * tile, (i + 1) * tile)
@@ -1505,7 +1532,7 @@
             jax.ShapeDtypeStruct((per_core, rows_in, half), FULL),
             jax.ShapeDtypeStruct((5, 128), FULL),
         ),
-        in_specs=[vmem] * 3 + [anywhere] * 3 + [vmem] * 5 + [anywhere],
+        in_specs=[vmem] * 3 + [anywhere] * 9,
         out_specs=[vmem] * 7,
         scratch_shapes=[
             low(units + (unit, hidden)),
@@ -1546,6 +1573,12 @@
             low((2, nz + 1, slabs, unit, half)),
             full((parts, 5, 128)),
             full((parts, 5, 128)),
+            low((length, head)),
+            low((length, head)),
+            low((length, head)),
+            full((head, length)),
+            full((1, length)),
+            DMA((5,)),
             DMA((8,)),
             DMA((8,)),
             DMA((8,)),

time: 270 us -> 267 us (0.989)
  Pallas kernels: 257 us -> 254 us
where the time goes in v2:
time: 267 us; the launch traced here: 263 us
  Pallas kernels  254 us (95%)
  local copies, waits for them, and re-layouts  3.66 us (1%)
    pallas_call x1, Pallas kernels, rest(): pl.pallas_call(partial(rest_kernel, nz, 512), out_shape=(jax.ShapeDtypeSt...  158 us
    pallas_call x1, Pallas kernels, attend(): pl.pallas_call(partial(attend_kernel, nz, ny), out_shape=(jax.ShapeDtypeS...  89.3 us
    pallas_call x1, Pallas kernels, finish(): pl.pallas_call(partial(finish_kernel, nz), out_shape=(jax.ShapeDtypeStruc...  6.28 us
  transfers between devices with their start and end apart: 2, of which 1 were waited for; matrix products, arithmetic and copies ran while one was open for 1% of the time, Pallas kernels for 0%

profile of v2, /device:TPU:11, one launch (start us, length us, event | category | flops | bytes accessed | tf_op | source)
XLA Modules:
  0.0 263.0 jit_solution(6360124392987305811)
XLA Ops:
  0.6 1.1 reshape.73
  1.8 0.2 reshape.74
  2.0 0.7 collective-permute-start.1
  2.8 0.9 pad_add_fusion
  3.6 0.8 copy.53
  4.4 1.1 reshape.68
  5.5 0.2 copy.50
  5.6 0.2 reshape_reshape.3
  5.9 0.1 collective-permute-start
  6.0 0.0 collective-permute-done.1
  6.2 1.1 collective-permute-done
  7.4 0.7 pad_maximum_fusion.3.mw_ref
  8.0 0.7 pad_maximum_fusion.up_ref
  8.7 89.3 %attend.1 = (bf16[4,2,2,160,384]{4,3,2,1,0:T(8,128)(2,1)}, bf16[4,2,2,5,48,384]{5,4,3,2,1,0:T(8,128)(2,1)}, bf16[4,2,2,96,768]{4,3,2,1,0:T(8,128)(2,1)}, bf16[20...) custom-call(bf16[128,768]{1,0:T(8,128)(2,1)} %bitcast.72, ...), custom_call_target="tpu_custom_call" | custom-call | flops 1610612736 | bytes 12582912 | tf_op jit(solution)/shard_map/attend/pallas_call | solution.py:707
  98.1 158.4 %rest.1 = (bf16[2,128,768]{2,1,0:T(8,128)(2,1)}, f32[2,128,768]{2,1,0:T(8,128)}, f32[2,9,48,384]{3,2,1,0:T(8,128)}, f32[2,5,24,384]{3,2,1,0:T(8,128)}, f32[6,48,...) custom-call(bf16[256,768]{1,0:T(8,128)(2,1)} %bitcast.74, ...), custom_call_target="tpu_custom_call" | custom-call | flops 18119393280 | bytes 70778880 | tf_op jit(solution)/shard_map/rest/pallas_call | solution.py:1524
  256.5 6.3 %finish.1 = (bf16[2,128,768]{2,1,0:T(8,128)(2,1)}, f32[2,128,768]{2,1,0:T(8,128)}, f32[2,24]{1,0:T(2,128)}, f32[2,24]{1,0:T(2,128)}, f32[2,24,2304]{2,1,0:T(8,12...) custom-call(bf16[2,128,768]{2,1,0:T(8,128)(2,1)} %get-tuple-element., ...), custom_call_target="tpu_custom_call" | custom-call | tf_op jit(solution)/shard_map/finish/pallas_call | solution.py:1496
  (16 shorter events, 0.3 us)
Async XLA Ops:
  2.0 4.0 %collective-permute-start.1 = (bf16[24,1536]{1,0:T(8,128)(2,1)S(1)}, bf16[24,1536]{1,0:T(8,128)(2,1)S(1)}, u32[]{:S(2)}, u32[]{:S(2)}) collective-permute-start(bf16[24,1536]{1,0:T(8,128)(2,1)S(1)} %dynamic-slice_bitcast_fusion.1), channel_id=1, source_target_pairs={{0,2},{1,3},{2,0},{3,1},{4,6},{5,7},{6,4},{7,5},{8,10},{9,11},{10,... | collective-permute-start | bytes 221192 | tf_op jit(solution)/shard_map/ppermute | solution.py:68
  5.9 1.3 collective-permute-start
